TPU v7x, 32 devices: a whole 2x2x4 slice. The times are simulated.
32 devices in a mesh: groups: 2 (over y), expert: 4 (over z), tensor: 4 (over x, core).
Axes of the slice: x: 2, y: 2, z: 4, core: 2. Of those that a mesh axis runs over, the one named last changes fastest.
Arguments:
- hidden_in: bfloat16 [1536, 3072], P(('groups', 'expert'), 'tensor'), parts along dimension 0, may hold values from -81 to 81
- norm_gain: float32 [3072], P('tensor'), may hold values from 0.1 to 1.9
- router_weight: float32 [3072, 4], P('tensor'), may hold values from -0.109375 to 0.109375
- routes: int32 [1536, 2], P(('groups', 'expert')), parts along dimension 0, may hold values from 0 to 3, all different within a row; in each aligned block of 192 rows (0 to 191, 192 to 383, ...) at most 128 rows name the same one
- gate_weight: bfloat16 [4, 3072, 8192], P('expert', None, 'tensor'), may hold values from -0.109375 to 0.109375
- up_weight: bfloat16 [4, 3072, 8192], P('expert', None, 'tensor'), may hold values from -0.109375 to 0.109375
- down_weight: bfloat16 [4, 8192, 3072], P('expert', 'tensor'), may hold values from -0.0625 to 0.0625
- grad_out: bfloat16 [1536, 3072], P(('groups', 'expert'), 'tensor'), parts along dimension 0, may hold values from -6 to 6
Outputs:
- grad_input: bfloat16 [1536, 3072], P(('groups', 'expert'), 'tensor'), parts along dimension 0
- grad_gain: float32 [6144], P(('groups', 'tensor')), parts along dimension 0
- grad_router: float32 [6144, 4], P(('groups', 'tensor')), parts along dimension 0
- grad_down: bfloat16 [8, 8192, 3072], P(('groups', 'expert'), 'tensor'), parts along dimension 0
There are 2 independent parts, one for each index of `groups`. A program takes and returns all parts, laid end to end along the dimension named above; an argument that names none is the same for every part. Nothing has to cross between parts.
Inputs may be any that keep to these rules, and one draw needn't show every extreme that they name: `routes`: each row names two different experts. Within the rows of one device no expert is named by more than 128 rows, and in every draw some expert is named by exactly 128 rows of some device.
All inputs are finite; a program needn't handle non-finite values.
Results may differ from a plain program's by a relative error of at most 0.0076.
Values may be sent and summed in bfloat16 or wider, within the bound.
A program may use at most 192 MiB of HBM per device.

v0:
```python
import jax
import jax.numpy as jnp
from jax import lax
from jax.sharding import PartitionSpec as P

EPS = 1e-05
PRECISE = lax.Precision.HIGHEST


def body(
    hidden_in, norm_gain, router_weight, routes, gate_weight, up_weight, down_weight, grad_out
):
    tok_rows, part_cols = hidden_in.shape
    expert_count = router_weight.shape[1]
    feat_width = part_cols * lax.axis_size("tensor")
    capacity = 8 * tok_rows // (3 * expert_count)
    inputs_f = hidden_in.astype(jnp.float32)
    scaled_in = inputs_f * norm_gain[None, :]
    square_part = jnp.sum(inputs_f * inputs_f, axis=1)
    logit_part = jnp.dot(scaled_in, router_weight, precision=PRECISE)
    square_sum, logit_sum = lax.psum((square_part, logit_part), "tensor")
    inv_rms = lax.rsqrt(square_sum / feat_width + EPS)[:, None]
    normed = scaled_in * inv_rms
    normed_b = normed.astype(jnp.bfloat16)
    logits = logit_sum * inv_rms
    labels = jnp.arange(expert_count, dtype=jnp.int32)
    first_hot = (routes[:, 0:1] == labels[None, :]).astype(jnp.float32)
    second_hot = (routes[:, 1:2] == labels[None, :]).astype(jnp.float32)
    prob_first = jax.nn.sigmoid(jnp.sum(logits * (first_hot - second_hot), axis=1))
    prob_second = 1.0 - prob_first
    flat_routes = routes.reshape(-1)
    route_hot = (flat_routes[:, None] == labels[None, :]).astype(jnp.int32)
    slot_rank = jnp.sum(
        (jnp.cumsum(route_hot, axis=0, dtype=jnp.int32) - route_hot) * route_hot,
        axis=1,
        dtype=jnp.int32,
    )
    slot_index = (flat_routes * capacity + slot_rank).reshape(tok_rows, 2)
    slot_ids = jnp.arange(expert_count * capacity, dtype=jnp.int32)
    pick_first = (slot_index[:, 0:1] == slot_ids[None, :]).astype(jnp.float32)
    pick_second = (slot_index[:, 1:2] == slot_ids[None, :]).astype(jnp.float32)
    pick_both = pick_first + pick_second
    pick_bf = pick_both.astype(jnp.bfloat16)
    weight_slots = jnp.dot(prob_first, pick_first, precision=PRECISE) + jnp.dot(
        prob_second, pick_second, precision=PRECISE
    )
    weight_slots = weight_slots.astype(jnp.bfloat16).reshape(expert_count, capacity)

    def dispatch(row_block):
        placed = jnp.einsum("ts,td->sd", pick_bf, row_block, preferred_element_type=jnp.float32)
        return placed.astype(jnp.bfloat16).reshape(expert_count, capacity, row_block.shape[1])

    send_rows = dispatch(normed_b)
    send_grads = dispatch(grad_out)
    got_rows, got_grads, got_weight = (
        lax.all_to_all(send_rows, "expert", split_axis=0, concat_axis=0, tiled=True),
        lax.all_to_all(send_grads, "expert", split_axis=0, concat_axis=0, tiled=True),
        lax.all_to_all(weight_slots, "expert", split_axis=0, concat_axis=0, tiled=True),
    )
    full_rows, full_grads = (
        lax.all_gather(got_rows, "tensor", axis=2, tiled=True),
        lax.all_gather(got_grads, "tensor", axis=2, tiled=True),
    )
    slot_total = full_rows.shape[0] * capacity
    slot_rows = full_rows.reshape(slot_total, feat_width)
    slot_grads = full_grads.reshape(slot_total, feat_width)
    gate_matrix = gate_weight[0]
    up_matrix = up_weight[0]
    down_matrix = down_weight[0]
    gate_pre = jnp.dot(slot_rows, gate_matrix, preferred_element_type=jnp.float32)
    up_pre = jnp.dot(slot_rows, up_matrix, preferred_element_type=jnp.float32)
    gate_sig = jax.nn.sigmoid(gate_pre)
    hidden_act = (gate_pre * gate_sig * up_pre).astype(jnp.bfloat16)
    expert_out = jnp.dot(hidden_act, down_matrix, preferred_element_type=jnp.float32)
    prob_part = jnp.sum(slot_grads.astype(jnp.float32) * expert_out, axis=1)
    out_grad = (
        got_weight.reshape(slot_total).astype(jnp.float32)[:, None] * slot_grads.astype(jnp.float32)
    ).astype(jnp.bfloat16)
    grad_down = jnp.einsum(
        "sf,sd->fd", hidden_act, out_grad, preferred_element_type=jnp.float32
    ).astype(jnp.bfloat16)[None]
    act_grad = jnp.einsum("sd,fd->sf", out_grad, down_matrix, preferred_element_type=jnp.float32)
    gate_grad = (act_grad * up_pre * gate_sig * (1.0 + gate_pre * (1.0 - gate_sig))).astype(
        jnp.bfloat16
    )
    up_grad = (act_grad * gate_pre * gate_sig).astype(jnp.bfloat16)
    row_part = jnp.einsum("sf,df->sd", gate_grad, gate_matrix, preferred_element_type=jnp.float32)
    row_part = row_part + jnp.einsum(
        "sf,df->sd", up_grad, up_matrix, preferred_element_type=jnp.float32
    )
    tensor_pos = lax.axis_index("tensor")
    row_sums, prob_grad = lax.psum((row_part, prob_part), "tensor")
    inner_sum = jnp.sum(slot_rows.astype(jnp.float32) * row_sums, axis=1)
    row_own = lax.dynamic_slice_in_dim(row_sums, tensor_pos * part_cols, part_cols, 1)
    back_rows, back_inner, back_prob = (
        lax.all_to_all(
            row_own.reshape(-1, capacity, part_cols),
            "expert",
            split_axis=0,
            concat_axis=0,
            tiled=True,
        ),
        lax.all_to_all(
            inner_sum.reshape(-1, capacity), "expert", split_axis=0, concat_axis=0, tiled=True
        ),
        lax.all_to_all(
            prob_grad.reshape(-1, capacity), "expert", split_axis=0, concat_axis=0, tiled=True
        ),
    )
    back_rows = back_rows.reshape(expert_count * capacity, part_cols)
    back_inner = back_inner.reshape(-1)
    back_prob = back_prob.reshape(-1)
    expert_grad = jnp.dot(pick_both, back_rows, precision=PRECISE)
    token_inner = jnp.dot(pick_both, back_inner, precision=PRECISE)
    prob_grad_first = jnp.dot(pick_first, back_prob, precision=PRECISE)
    prob_grad_second = jnp.dot(pick_second, back_prob, precision=PRECISE)
    gap_grad = (prob_grad_first - prob_grad_second) * prob_first * prob_second
    logit_grad = gap_grad[:, None] * (first_hot - second_hot)
    total_grad = expert_grad + jnp.einsum("te,de->td", logit_grad, router_weight, precision=PRECISE)
    norm_dot = (token_inner + jnp.sum(logits * logit_grad, axis=1)) / inv_rms[:, 0]
    cubed = inv_rms * inv_rms * inv_rms
    grad_input = (
        inv_rms * norm_gain[None, :] * total_grad
        - inputs_f * cubed * (norm_dot[:, None] / feat_width)
    ).astype(jnp.bfloat16)
    gain_part = jnp.sum(total_grad * inputs_f * inv_rms, axis=0)
    router_part = jnp.einsum("td,te->de", normed, logit_grad, precision=PRECISE)
    grad_gain, grad_router = lax.psum((gain_part, router_part), "expert")
    return (grad_input, grad_gain, grad_router, grad_down)


def solution(mesh):
    placed = (
        P(("groups", "expert"), "tensor"),
        P("tensor"),
        P("tensor", None),
        P(("groups", "expert"), None),
        P("expert", None, "tensor"),
        P("expert", None, "tensor"),
        P("expert", "tensor", None),
        P(("groups", "expert"), "tensor"),
    )
    return jax.shard_map(
        body,
        mesh=mesh,
        in_specs=placed,
        out_specs=(
            P(("groups", "expert"), "tensor"),
            P(("groups", "tensor")),
            P(("groups", "tensor"), None),
            P(("groups", "expert"), "tensor", None),
        ),
        check_vma=False,
    )
```

profile of v0, /device:TPU:0, one launch (start us, length us, event | category | flops | bytes accessed | tf_op | source)
XLA Modules:
  0.0 386.5 jit_solution(16108113818905220846)
XLA Ops:
  7.2 0.0 copy-start
  7.2 0.0 copy-start.7
  7.2 0.0 copy-start.4
  7.2 0.0 copy-start.9
  7.2 0.0 all-gather.5.cloned.1.call-start
  7.3 0.9 copy.29
  8.1 0.1 eq.89
  8.3 0.1 eq.85
  8.4 1.1 fusion.27
  9.5 8.3 %psum.42 = f32[192]{0:T(256)S(1)} all-reduce(f32[192]{0:T(256)S(1)} %fusion.27), channel_id=1, replica_groups=mesh['groups'=2,'expert'=4,'tensor'=4] {'tensor'}, use_global_device_ids=true, to_apply=%region_1.0 | all-reduce | flops 192 | bytes 1536 | tf_op jit(solution)/shard_map/psum | solution.py:21
  17.9 1.2 reduce-window.6
  19.1 0.2 slice_reduce_fusion
  19.3 0.2 reduce-window.9
  19.5 0.1 add_bitcast_fusion
  19.6 0.1 reduce_sum.67
  19.8 0.1 copy.31
  19.8 0.7 multiply_add_fusion
  20.5 1.5 convolution_convert_fusion
  22.0 23.7 %all_to_all.42 = bf16[4,128,768]{2,1,0:T(8,128)(2,1)} all-to-all(bf16[4,128,768]{2,1,0:T(8,128)(2,1)S(1)} %bitcast.102), channel_id=1, replica_groups=mesh['groups'=2,'expert'=4,'tensor'=4] {'expert'}, dimensions={0} | all-to-all | bytes 1572864 | tf_op jit(solution)/shard_map/all_to_all | solution.py:56
  45.7 0.0 all-gather.5.cloned.1.call-update
  45.7 0.0 all-gather.3.cloned.1.call-start
  45.8 0.5 convolution_convert_fusion.1
  46.3 22.2 %all_to_all.43 = bf16[4,128,768]{2,1,0:T(8,128)(2,1)} all-to-all(bf16[4,128,768]{2,1,0:T(8,128)(2,1)S(1)} %bitcast.103), channel_id=1, replica_groups=mesh['groups'=2,'expert'=4,'tensor'=4] {'expert'}, dimensions={0} | all-to-all | bytes 1572864 | tf_op jit(solution)/shard_map/all_to_all | solution.py:57
  68.5 0.0 all-gather.3.cloned.1.call-update
  68.6 0.6 fusion.23
  69.1 4.5 %all-gather.5.cloned.1.call-done = bf16[4,128,3072]{2,1,0:T(8,128)(2,1)} async-done(((bf16[4,128,768]{2,1,0:T(8,128)(2,1)}), bf16[4,128,3072]{2,1,0:T(8,128)(2,1)}) %all-gather.5.cloned.1.call-update) | async-done | bytes 3145744 | tf_op jit(solution)/shard_map/all_gather | solution.py:61
  73.6 12.4 %fusion.2 = f32[512,2048]{1,0:T(8,128)S(1)} fusion(bf16[512,3072]{1,0:T(8,128)(2,1)} %bitcast.99, bf16[1,3072,2048]{2,1,0:T(8,128)(2,1)} %param.12), kind=kOutput, calls=%fused_computation.2 | convolution fusion | flops 6442450944 | bytes 19922944 | tf_op jit(solution)/shard_map/dot_general | solution.py:70
  86.0 0.0 copy-start.10
  86.0 2.0 copy-done.10
  88.0 11.5 %multiply_convert_fusion = (bf16[512,2048]{1,0:T(8,128)(2,1)}, f32[512,2048]{1,0:T(8,128)}) fusion(f32[512,2048]{1,0:T(8,128)S(1)} %fusion.2, bf16[512,3072]{1,0:T(8,128)(2,1)S(1)} %bitcast.100, bf16[1,3072,2048]{2,1,0:T(8,128)(2,1)} %param.13), kind=kOutput, calls=%fused_computation.21 | convolution fusion | flops 6448742400 | bytes 26214400 | tf_op jit(solution)/shard_map/dot_general | solution.py:71
  99.5 4.2 %all-gather.3.cloned.1.call-done = bf16[4,128,3072]{2,1,0:T(8,128)(2,1)} async-done(((bf16[4,128,768]{2,1,0:T(8,128)(2,1)}), bf16[4,128,3072]{2,1,0:T(8,128)(2,1)}) %all-gather.3.cloned.1.call-update) | async-done | bytes 3145744 | tf_op jit(solution)/shard_map/all_gather | solution.py:62
  103.7 12.5 %fusion.13 = f32[512]{0:T(512)S(1)} fusion(bf16[4,128,3072]{2,1,0:T(8,128)(2,1)} %all-gather.3.cloned.1.call-done, bf16[512,2048]{1,0:T(8,128)(2,1)} %get-tuple-element.18, bf16[1,2048,3072]{2,1,0:T(8,128)(2,1)} %param.14), kind=kOutput, calls=%fused_computation.17 | convolution fusion | flops 6447169024 | bytes 17827840 | tf_op jit(solution)/shard_map/dot_general | solution.py:74
  116.2 6.6 %all-reduce = (f32[192,4]{0,1:T(4,128)S(1)}, f32[4,1,128]{2,1,0:T(1,128)}) all-reduce(f32[192,4]{0,1:T(4,128)S(1)} %fusion.23, f32[4,1,128]{2,1,0:T(1,128)S(1)} %bitcast.128), channel_id=1, replica_groups=mesh['groups'=2,'expert'=4,'tensor'=4] {'tensor'}, use_global_device_ids=true, to_apply=%region_5.6 | all-reduce | flops 1280 | bytes 10240 | tf_op jit(solution)/shard_map/psum | solution.py:21
  122.8 4.8 %all-to-all-start.4 = ((f32[4,1,128]{2,1,0:T(1,128)}), f32[4,1,128]{2,1,0:T(1,128)S(1)}, u32[]{:S(2)}, u32[]{:S(2)}) async-start(f32[4,1,128]{2,1,0:T(1,128)} %get-tuple-element.5), calls=%async_computation.4 | async-start | bytes 4096 | tf_op jit(solution)/shard_map/all_to_all | solution.py:106
  127.6 5.4 %all-to-all-done.4 = f32[4,1,128]{2,1,0:T(1,128)S(1)} async-done(((f32[4,1,128]{2,1,0:T(1,128)}), f32[4,1,128]{2,1,0:T(1,128)S(1)}, u32[]{:S(2)}, u32[]{:S(2)}) %all-to-all-start.4) | async-done | bytes 2080 | tf_op jit(solution)/shard_map/all_to_all | solution.py:106
  133.0 0.3 fusion.38
  133.3 0.4 fusion.33
  133.7 0.3 fusion.39
  134.0 0.3 fusion.34
  134.4 7.9 %all_to_all.44 = bf16[4,1,128]{2,1,0:T(2,128)(2,1)S(1)} all-to-all(bf16[4,1,128]{2,1,0:T(2,128)(2,1)S(1)} %copy.32), channel_id=1, replica_groups=mesh['groups'=2,'expert'=4,'tensor'=4] {'expert'}, dimensions={0} | all-to-all | bytes 2048 | tf_op jit(solution)/shard_map/all_to_all | solution.py:58
  142.2 0.0 copy-done.2
  142.2 1.0 fusion.12
  143.2 0.0 copy-start.11
  143.2 11.2 %fusion.10 = f32[512,2048]{1,0:T(8,128)} fusion(bf16[512,3072]{1,0:T(8,128)(2,1)S(1)} %bitcast.101, bf16[1,2048,3072]{2,1,0:T(8,128)(2,1)} %param.14), kind=kOutput, calls=%fused_computation.10 | convolution fusion | flops 6442450944 | bytes 19922944 | tf_op jit(solution)/shard_map/sd,fd->sf/dot_general | solution.py:82
  154.4 0.0 copy-done.11
  154.4 16.1 %fusion = f32[512,3072]{1,0:T(8,128)} fusion(bf16[1,3072,2048]{2,1,0:T(8,128)(2,1)} %param.12, f32[512,2048]{1,0:T(8,128)S(1)} %copy-done.11, f32[512,2048]{1,0:T(8,128)} %fusion.10, f32[512,2048]{1,0:T(8,128)} %get-tuple-element.19), kind=kOutput, calls=%fused_computation | convolution fusion | flops 6452936704 | bytes 31457280 | tf_op jit(solution)/shard_map/sf,df->sd/dot_general | solution.py:87
  170.5 14.9 %fusion.17 = f32[512,3072]{1,0:T(8,128)} fusion(f32[512,3072]{1,0:T(8,128)} %fusion, bf16[1,3072,2048]{2,1,0:T(8,128)(2,1)} %param.13, f32[512,2048]{1,0:T(8,128)} %fusion.10, f32[512,2048]{1,0:T(8,128)S(1)} %copy-done.11), kind=kOutput, calls=%fused_computation.20 | convolution fusion | flops 6450315264 | bytes 33554432 | tf_op jit(solution)/shard_map/sf,df->sd/dot_general | solution.py:88
  185.4 0.0 all-reduce.4.cloned.1.call-update
  185.4 0.9 copy-done.5
  186.3 0.5 fusion.24
  186.8 116.4 %all-reduce.4.cloned.1.call-done = f32[512,3072]{1,0:T(8,128)} async-done(((f32[512,3072]{1,0:T(8,128)}), f32[512,3072]{1,0:T(8,128)}) %all-reduce.4.cloned.1.call-update) | async-done | bytes 6291472 | tf_op jit(solution)/shard_map/psum | solution.py:92
  303.2 5.0 %multiply_reduce_fusion = f32[512]{0:T(512)} fusion(f32[512,3072]{1,0:T(8,128)} %all-reduce.4.cloned.1.call-done, bf16[4,128,3072]{2,1,0:T(8,128)(2,1)} %all-gather.5.cloned.1.call-done), kind=kLoop, calls=%fused_computation.19 | loop fusion | flops 4718080 | bytes 9439232 | tf_op jit(solution)/shard_map/reduce_sum | solution.py:93
  308.2 4.6 %all-to-all-start.5 = ((f32[4,1,128]{2,1,0:T(1,128)}), f32[4,1,128]{2,1,0:T(1,128)S(1)}, u32[]{:S(2)}, u32[]{:S(2)}) async-start(f32[4,1,128]{2,1,0:T(1,128)} %bitcast.27), calls=%async_computation.5 | async-start | bytes 4096 | tf_op jit(solution)/shard_map/all_to_all | solution.py:103
  312.8 2.7 constant_dynamic-slice_fusion
  315.5 2.8 all-to-all-done.5
  318.3 4.6 %all-to-all-start.3 = ((f32[4,128,768]{2,1,0:T(8,128)}), f32[4,128,768]{2,1,0:T(8,128)}, u32[]{:S(2)}, u32[]{:S(2)}) async-start(f32[4,128,768]{2,1,0:T(8,128)} %bitcast.98), calls=%async_computation.3 | async-start | bytes 3145728 | tf_op jit(solution)/shard_map/all_to_all | solution.py:96
  322.9 1.0 fusion.14
  323.9 0.6 copy-done.12
  324.5 9.7 %convert_bitcast_fusion = bf16[1,2048,3072]{2,1,0:T(8,128)(2,1)} fusion(bf16[512,2048]{1,0:T(8,128)(2,1)S(1)} %copy-done.12, bf16[512,3072]{1,0:T(8,128)(2,1)S(1)} %fusion.14), kind=kOutput, calls=%fused_computation.12 | convolution fusion | flops 6448742400 | bytes 17825792 | tf_op jit(solution)/shard_map/sf,sd->fd/dot_general | solution.py:79
  334.1 0.5 fusion.35
  334.7 23.6 %all-to-all-done.3 = f32[4,128,768]{2,1,0:T(8,128)} async-done(((f32[4,128,768]{2,1,0:T(8,128)}), f32[4,128,768]{2,1,0:T(8,128)}, u32[]{:S(2)}, u32[]{:S(2)}) %all-to-all-start.3) | async-done | bytes 1572896 | tf_op jit(solution)/shard_map/all_to_all | solution.py:96
  358.3 2.7 fusion.36
  361.0 1.6 fusion.32
  362.5 17.4 %all-reduce.1 = (f32[768]{0:T(1024)}, f32[768,4]{0,1:T(4,128)}) all-reduce(f32[768]{0:T(1024)S(1)} %get-tuple-element.10, f32[768,4]{0,1:T(4,128)S(1)} %fusion.24), channel_id=1, replica_groups=mesh['groups'=2,'expert'=4,'tensor'=4] {'expert'}, use_global_device_ids=true, to_apply=%region_13.14 | all-reduce | flops 3840 | bytes 30720 | tf_op jit(solution)/shard_map/psum | solution.py:128
  (29 shorter events, 0.2 us)
Async XLA Ops:
  7.2 38.6 %copy-start = (bf16[192,768]{1,0:T(8,128)(2,1)S(1)}, bf16[192,768]{1,0:T(8,128)(2,1)}, u32[]{:S(2)}) copy-start(bf16[192,768]{1,0:T(8,128)(2,1)} %param.15) | copy-start | bytes 884740
  7.2 61.3 %copy-start.7 = (s32[192,2]{0,1:T(2,128)S(1)}, s32[192,2]{0,1:T(2,128)}, u32[]{:S(2)}) copy-start(s32[192,2]{0,1:T(2,128)} %param.11) | copy-start | bytes 4612
  7.2 61.3 %copy-start.4 = (bf16[192,768]{1,0:T(8,128)(2,1)S(1)}, bf16[192,768]{1,0:T(8,128)(2,1)}, u32[]{:S(2)}) copy-start(bf16[192,768]{1,0:T(8,128)(2,1)} %param.8) | copy-start | bytes 884740
  7.2 61.3 %copy-start.9 = (f32[768]{0:T(1024)S(1)}, f32[768]{0:T(1024)}, u32[]{:S(2)}) copy-start(f32[768]{0:T(1024)} %param.9) | copy-start | bytes 9220
  7.2 61.3 %copy-start.8 = (f32[768,4]{0,1:T(4,128)S(1)}, f32[768,4]{0,1:T(4,128)}, u32[]{:S(2)}) copy-start(f32[768,4]{0,1:T(4,128)} %param.10) | copy-start | bytes 36868
  7.2 66.3 %all-gather.5.cloned.1.call-start = ((), (), s32[]{:S(2)}) async-start(), calls=%async_computation.7 | async-start | bytes 3932160 | tf_op jit(solution)/shard_map/all_gather | solution.py:61
  45.7 58.0 %all-gather.3.cloned.1.call-start = ((), (), s32[]{:S(2)}) async-start(), calls=%async_computation.6 | async-start | bytes 3932160 | tf_op jit(solution)/shard_map/all_gather | solution.py:62
  73.6 14.4 %copy-start.3 = (bf16[4,128,3072]{2,1,0:T(8,128)(2,1)S(1)}, bf16[4,128,3072]{2,1,0:T(8,128)(2,1)}, u32[]{:S(2)}) copy-start(bf16[4,128,3072]{2,1,0:T(8,128)(2,1)} %all-gather.5.cloned.1.call-done) | copy-start | bytes 9437188
  86.0 2.0 copy-start.10
  103.7 38.5 %copy-start.2 = (bf16[4,128,3072]{2,1,0:T(8,128)(2,1)S(1)}, bf16[4,128,3072]{2,1,0:T(8,128)(2,1)}, u32[]{:S(2)}) copy-start(bf16[4,128,3072]{2,1,0:T(8,128)(2,1)} %all-gather.3.cloned.1.call-done) | copy-start | bytes 9437188
  122.8 10.2 %all-to-all-start.4 = ((f32[4,1,128]{2,1,0:T(1,128)}), f32[4,1,128]{2,1,0:T(1,128)S(1)}, u32[]{:S(2)}, u32[]{:S(2)}) async-start(f32[4,1,128]{2,1,0:T(1,128)} %get-tuple-element.5), calls=%async_computation.4 | async-start | bytes 4096 | tf_op jit(solution)/shard_map/all_to_all | solution.py:106
  127.5 175.7 %all-reduce.4.cloned.1.call-start = ((), (), s32[]{:S(2)}) async-start(), calls=%async_computation.8 | async-start | bytes 12582912 | tf_op jit(solution)/shard_map/psum | solution.py:92
  143.2 11.2 %copy-start.11 = (f32[512,2048]{1,0:T(8,128)S(1)}, f32[512,2048]{1,0:T(8,128)}, u32[]{:S(2)}) copy-start(f32[512,2048]{1,0:T(8,128)} %copy-done.10) | copy-start | bytes 12582916
  185.3 1.0 copy-start.5
  308.2 10.1 %all-to-all-start.5 = ((f32[4,1,128]{2,1,0:T(1,128)}), f32[4,1,128]{2,1,0:T(1,128)S(1)}, u32[]{:S(2)}, u32[]{:S(2)}) async-start(f32[4,1,128]{2,1,0:T(1,128)} %bitcast.27), calls=%async_computation.5 | async-start | bytes 4096 | tf_op jit(solution)/shard_map/all_to_all | solution.py:103
  318.3 40.0 %all-to-all-start.3 = ((f32[4,128,768]{2,1,0:T(8,128)}), f32[4,128,768]{2,1,0:T(8,128)}, u32[]{:S(2)}, u32[]{:S(2)}) async-start(f32[4,128,768]{2,1,0:T(8,128)} %bitcast.98), calls=%async_computation.3 | async-start | bytes 3145728 | tf_op jit(solution)/shard_map/all_to_all | solution.py:96
  322.9 1.6 copy-start.12
  324.5 36.5 %copy-start.6 = (bf16[192,768]{1,0:T(8,128)(2,1)S(1)}, bf16[192,768]{1,0:T(8,128)(2,1)}, u32[]{:S(2)}) copy-start(bf16[192,768]{1,0:T(8,128)(2,1)} %param.8) | copy-start | bytes 884740
  324.5 55.5 %copy-start.1 = (bf16[192,768]{1,0:T(8,128)(2,1)S(1)}, bf16[192,768]{1,0:T(8,128)(2,1)}, u32[]{:S(2)}) copy-start(bf16[192,768]{1,0:T(8,128)(2,1)} %param.15) | copy-start | bytes 884740
Sparse Core Ops, SparseCore 0:
  45.9 27.6 all-gather.4
  75.1 28.5 all-gather.2
  185.5 117.7 all-reduce.3
where the time goes:
time: 387 us
  waiting for transfers between devices  157 us (41%)
  matrix products  97.3 us (25%)
  blocking collectives  86.1 us (22%)
  starting transfers between devices  14 us (4%)
  between operations  14 us (4%)
  other arithmetic  10.3 us (3%)
  local copies, waits for them, and re-layouts  7.82 us (2%)
    psum x1, waiting for transfers between devices, body(): row_sums, prob_grad = lax.psum((row_part, prob_part), 'tensor')  116 us
    all_to_all x1, blocking collectives, body(): lax.all_to_all(send_rows, 'expert', split_axis=0, concat_axis=0, tiled=True)  23.7 us
    all_to_all x1, waiting for transfers between devices, body(): lax.all_to_all(row_own.reshape(-1, capacity, part_cols), 'expert', split_...  23.6 us
    all_to_all x1, blocking collectives, body(): lax.all_to_all(send_grads, 'expert', split_axis=0, concat_axis=0, tiled=T...  22.2 us
    psum x1, blocking collectives, body(): grad_gain, grad_router = lax.psum((gain_part, router_part), 'expert')  17.4 us
    dot_general x1, matrix products, body(): jnp.einsum('sf,df->sd', gate_grad, gate_matrix, preferred_element_type=jn...  16.1 us
    psum x2, blocking collectives, body(): square_sum, logit_sum = lax.psum((square_part, logit_part), 'tensor')  14.9 us
    dot_general x1, matrix products, body(): jnp.einsum('sf,df->sd', up_grad, up_matrix, preferred_element_type=jnp.fl...  14.9 us
  transfers between devices with their start and end apart: 6, of which 6 were waited for; matrix products, arithmetic and copies ran while one was open for 10% of the time, Pallas kernels for 0%

commit v1 on v0

--- a/solution.py
+++ b/solution.py
@@ -41,29 +41,26 @@
     pick_second = (slot_index[:, 1:2] == slot_ids[None, :]).astype(jnp.float32)
     pick_both = pick_first + pick_second
     pick_bf = pick_both.astype(jnp.bfloat16)
-    weight_slots = jnp.dot(prob_first, pick_first, precision=PRECISE) + jnp.dot(
-        prob_second, pick_second, precision=PRECISE
-    )
-    weight_slots = weight_slots.astype(jnp.bfloat16).reshape(expert_count, capacity)
+    prob_first_b = prob_first.astype(jnp.bfloat16)
+    prob_second_b = prob_second.astype(jnp.bfloat16)
+    pick_weight = (
+        pick_first * prob_first_b.astype(jnp.float32)[:, None]
+        + pick_second * prob_second_b.astype(jnp.float32)[:, None]
+    ).astype(jnp.bfloat16)
 
-    def dispatch(row_block):
-        placed = jnp.einsum("ts,td->sd", pick_bf, row_block, preferred_element_type=jnp.float32)
+    def dispatch(pick, row_block):
+        placed = jnp.einsum("ts,td->sd", pick, row_block, preferred_element_type=jnp.float32)
         return placed.astype(jnp.bfloat16).reshape(expert_count, capacity, row_block.shape[1])
 
-    send_rows = dispatch(normed_b)
-    send_grads = dispatch(grad_out)
-    got_rows, got_grads, got_weight = (
-        lax.all_to_all(send_rows, "expert", split_axis=0, concat_axis=0, tiled=True),
-        lax.all_to_all(send_grads, "expert", split_axis=0, concat_axis=0, tiled=True),
-        lax.all_to_all(weight_slots, "expert", split_axis=0, concat_axis=0, tiled=True),
-    )
-    full_rows, full_grads = (
-        lax.all_gather(got_rows, "tensor", axis=2, tiled=True),
-        lax.all_gather(got_grads, "tensor", axis=2, tiled=True),
-    )
-    slot_total = full_rows.shape[0] * capacity
-    slot_rows = full_rows.reshape(slot_total, feat_width)
-    slot_grads = full_grads.reshape(slot_total, feat_width)
+    send_grads = dispatch(pick_weight, grad_out)
+    send_rows = dispatch(pick_bf, normed_b)
+    got_rows = lax.all_to_all(send_rows, "expert", split_axis=0, concat_axis=0, tiled=True)
+    got_grads = lax.all_to_all(send_grads, "expert", split_axis=0, concat_axis=0, tiled=True)
+    slot_total = got_rows.shape[0] * capacity
+    slot_rows = lax.all_gather(got_rows, "tensor", axis=2, tiled=True)
+    slot_rows = slot_rows.reshape(slot_total, feat_width)
+    out_grad = lax.all_gather(got_grads, "tensor", axis=2, tiled=True)
+    out_grad = out_grad.reshape(slot_total, feat_width)
     gate_matrix = gate_weight[0]
     up_matrix = up_weight[0]
     down_matrix = down_weight[0]
@@ -71,11 +68,6 @@
     up_pre = jnp.dot(slot_rows, up_matrix, preferred_element_type=jnp.float32)
     gate_sig = jax.nn.sigmoid(gate_pre)
     hidden_act = (gate_pre * gate_sig * up_pre).astype(jnp.bfloat16)
-    expert_out = jnp.dot(hidden_act, down_matrix, preferred_element_type=jnp.float32)
-    prob_part = jnp.sum(slot_grads.astype(jnp.float32) * expert_out, axis=1)
-    out_grad = (
-        got_weight.reshape(slot_total).astype(jnp.float32)[:, None] * slot_grads.astype(jnp.float32)
-    ).astype(jnp.bfloat16)
     grad_down = jnp.einsum(
         "sf,sd->fd", hidden_act, out_grad, preferred_element_type=jnp.float32
     ).astype(jnp.bfloat16)[None]
@@ -88,33 +80,30 @@
     row_part = row_part + jnp.einsum(
         "sf,df->sd", up_grad, up_matrix, preferred_element_type=jnp.float32
     )
-    tensor_pos = lax.axis_index("tensor")
-    row_sums, prob_grad = lax.psum((row_part, prob_part), "tensor")
-    inner_sum = jnp.sum(slot_rows.astype(jnp.float32) * row_sums, axis=1)
-    row_own = lax.dynamic_slice_in_dim(row_sums, tensor_pos * part_cols, part_cols, 1)
-    back_rows, back_inner, back_prob = (
-        lax.all_to_all(
-            row_own.reshape(-1, capacity, part_cols),
-            "expert",
-            split_axis=0,
-            concat_axis=0,
-            tiled=True,
-        ),
-        lax.all_to_all(
-            inner_sum.reshape(-1, capacity), "expert", split_axis=0, concat_axis=0, tiled=True
-        ),
-        lax.all_to_all(
-            prob_grad.reshape(-1, capacity), "expert", split_axis=0, concat_axis=0, tiled=True
-        ),
+    prob_part = jnp.sum(hidden_act.astype(jnp.float32) * act_grad, axis=1)
+    inner_part = jnp.sum(
+        gate_grad.astype(jnp.float32) * gate_pre + up_grad.astype(jnp.float32) * up_pre, axis=1
     )
-    back_rows = back_rows.reshape(expert_count * capacity, part_cols)
-    back_inner = back_inner.reshape(-1)
-    back_prob = back_prob.reshape(-1)
-    expert_grad = jnp.dot(pick_both, back_rows, precision=PRECISE)
-    token_inner = jnp.dot(pick_both, back_inner, precision=PRECISE)
-    prob_grad_first = jnp.dot(pick_first, back_prob, precision=PRECISE)
-    prob_grad_second = jnp.dot(pick_second, back_prob, precision=PRECISE)
-    gap_grad = (prob_grad_first - prob_grad_second) * prob_first * prob_second
+    row_own = lax.psum_scatter(
+        row_part.astype(jnp.bfloat16), "tensor", scatter_dimension=1, tiled=True
+    )
+    back_rows = lax.all_to_all(
+        row_own.reshape(-1, capacity, part_cols), "expert", split_axis=0, concat_axis=0, tiled=True
+    ).reshape(expert_count * capacity, part_cols)
+    scalars = jnp.stack([inner_part, prob_part], axis=0).reshape(2, -1, capacity)
+    scalars = lax.all_to_all(scalars, "expert", split_axis=1, concat_axis=1, tiled=True)
+    scalars = scalars.reshape(2, expert_count * capacity)
+    pick_token = jnp.concatenate([pick_first, pick_second], axis=0)
+    token_scalars = jnp.einsum("cs,ts->ct", scalars, pick_token, precision=PRECISE)
+    token_scalars = lax.psum(token_scalars, "tensor").reshape(2, 2, tok_rows)
+    expert_grad = jnp.dot(pick_bf, back_rows, preferred_element_type=jnp.float32)
+    token_inner = token_scalars[0, 0] + token_scalars[0, 1]
+    ratio_first = prob_first / jnp.where(prob_first_b == 0, 1, prob_first_b).astype(jnp.float32)
+    ratio_second = prob_second / jnp.where(prob_second_b == 0, 1, prob_second_b).astype(jnp.float32)
+    gap_grad = (
+        token_scalars[1, 0] * ratio_first * prob_second
+        - token_scalars[1, 1] * ratio_second * prob_first
+    )
     logit_grad = gap_grad[:, None] * (first_hot - second_hot)
     total_grad = expert_grad + jnp.einsum("te,de->td", logit_grad, router_weight, precision=PRECISE)
     norm_dot = (token_inner + jnp.sum(logits * logit_grad, axis=1)) / inv_rms[:, 0]
@@ -125,7 +114,8 @@
     ).astype(jnp.bfloat16)
     gain_part = jnp.sum(total_grad * inputs_f * inv_rms, axis=0)
     router_part = jnp.einsum("td,te->de", normed, logit_grad, precision=PRECISE)
-    grad_gain, grad_router = lax.psum((gain_part, router_part), "expert")
+    sums = lax.psum(jnp.concatenate([gain_part[None, :], router_part.T], axis=0), "expert")
+    grad_gain, grad_router = sums[0], sums[1:].T
     return (grad_input, grad_gain, grad_router, grad_down)
 
 

time: 387 us -> 251 us (0.65)
  waiting for transfers between devices: 157 us -> 56 us
  matrix products: 97.3 us -> 86.6 us
  blocking collectives: 86.1 us -> 77.8 us
  other arithmetic: 10.3 us -> 4.14 us
  local copies, waits for them, and re-layouts: 7.82 us -> 2.95 us
  starting transfers between devices: 14 us -> 9.34 us
    psum x1 -> x0, waiting for transfers between devices: 116 us -> none  [body(): row_sums, prob_grad = lax.psum((row_part, prob_part), 'tensor')]
    dot_general x9 -> x4, matrix products: 19 us -> 3.89 us  [the longest x2 2.03 us: dispatch(): jnp.einsum('ts,td->sd', pick, row_block, preferred_element_type=jnp.float32)]
    all_gather x2, waiting for transfers between devices: 8.67 us -> 23.3 us  [the longest x1 18.3 us: body(): out_grad = lax.all_gather(got_grads, 'tensor', axis=2, tiled=True)]
    reduce_scatter x0 -> x1, waiting for transfers between devices: none -> 13.8 us  [body(): lax.psum_scatter(row_part.astype(jnp.bfloat16), 'tensor', scatter_dimensi...]
    all_to_all x2 -> x1, waiting for transfers between devices: 8.26 us -> 0.01 us  [body(): lax.all_to_all(scalars, 'expert', split_axis=1, concat_axis=1, tiled=True)]
    all_to_all x1 -> x0, blocking collectives: 7.89 us -> none  [body(): lax.all_to_all(weight_slots, 'expert', split_axis=0, concat_axis=0, tiled...]
    psum x2 -> x1, blocking collectives: 14.9 us -> 8.49 us  [body(): square_sum, logit_sum = lax.psum((square_part, logit_part), 'tensor')]
    psum x1 -> x2, blocking collectives: 17.4 us -> 23.6 us  [the longest x1 17.1 us: body(): lax.psum(jnp.concatenate([gain_part[None, :], router_part.T], axis=0), 'e...]
  transfers between devices with their start and end apart: 6 -> 5, of which waited for: 6 -> 4; matrix products, arithmetic and copies ran while one was open for 10% -> 11% of each run, Pallas kernels for 0% -> 0%
where the time goes in v1:
time: 251 us
  matrix products  86.6 us (35%)
  blocking collectives  77.8 us (31%)
  waiting for transfers between devices  56 us (22%)
  between operations  14 us (6%)
  starting transfers between devices  9.34 us (4%)
  other arithmetic  4.14 us (2%)
  local copies, waits for them, and re-layouts  2.95 us (1%)
    all_to_all x1, blocking collectives, body(): lax.all_to_all(send_rows, 'expert', split_axis=0, concat_axis=0, tiled=True)  23.6 us
    all_to_all x1, blocking collectives, body(): lax.all_to_all(send_grads, 'expert', split_axis=0, concat_axis=0, tiled=T...  22.1 us
    all_to_all x1, waiting for transfers between devices, body(): lax.all_to_all(row_own.reshape(-1, capacity, part_cols), 'expert', split_...  18.8 us
    all_gather x1, waiting for transfers between devices, body(): out_grad = lax.all_gather(got_grads, 'tensor', axis=2, tiled=True)  18.3 us
    psum x1, blocking collectives, body(): lax.psum(jnp.concatenate([gain_part[None, :], router_part.T], axis=0), 'e...  17.1 us
    dot_general x1, matrix products, body(): jnp.einsum('sf,df->sd', gate_grad, gate_matrix, preferred_element_type=jn...  16.3 us
    dot_general x1, matrix products, body(): up_pre = jnp.dot(slot_rows, up_matrix, preferred_element_type=jnp.float32)  15 us
    dot_general x1, matrix products, body(): jnp.einsum('sf,df->sd', up_grad, up_matrix, preferred_element_type=jnp.fl...  14.4 us
  transfers between devices with their start and end apart: 5, of which 4 were waited for; matrix products, arithmetic and copies ran while one was open for 11% of the time, Pallas kernels for 0%

profile of v1, /device:TPU:0, one launch (start us, length us, event | category | flops | bytes accessed | tf_op | source)
XLA Modules:
  0.0 250.8 jit_solution(453298821637018914)
XLA Ops:
  7.2 0.0 copy-start
  7.2 0.0 copy-start.4
  7.2 0.0 all-gather.5.cloned.1.call-start
  7.2 0.8 copy.24
  8.1 0.1 eq.103
  8.2 0.1 eq.99
  8.4 1.1 fusion.21
  9.5 1.5 fusion.17
  11.0 8.5 %all-reduce = (f32[192,4]{0,1:T(4,128)S(1)}, f32[192]{0:T(256)S(1)}) all-reduce(f32[192,4]{0,1:T(4,128)S(1)} %fusion.17, f32[192]{0:T(256)S(1)} %fusion.21), channel_id=1, replica_groups=mesh['groups'=2,'expert'=4,'tensor'=4] {'tensor'}, use_global_device_ids=true, to_apply=%region_5.6 | all-reduce | flops 960 | bytes 7680 | tf_op jit(solution)/shard_map/psum | solution.py:21
  19.5 1.2 reduce-window.6
  20.8 0.2 slice_reduce_fusion
  21.0 0.2 reduce-window.9
  21.2 0.1 add_bitcast_fusion
  21.3 0.1 reduce_sum.67
  21.4 0.1 copy.26
  21.5 0.7 multiply_add_fusion
  22.2 1.5 convolution_convert_fusion
  23.7 23.6 %all_to_all.20 = bf16[4,128,768]{2,1,0:T(8,128)(2,1)} all-to-all(bf16[4,128,768]{2,1,0:T(8,128)(2,1)S(1)} %bitcast.70), channel_id=1, replica_groups=mesh['groups'=2,'expert'=4,'tensor'=4] {'expert'}, dimensions={0} | all-to-all | bytes 1572864 | tf_op jit(solution)/shard_map/all_to_all | solution.py:57
  47.3 0.0 all-gather.5.cloned.1.call-update
  47.3 0.0 all-gather.3.cloned.1.call-start
  47.4 0.0 copy-done.4
  47.4 0.0 copy-done
  47.5 0.5 convolution_convert_fusion.1
  48.0 22.1 %all_to_all.21 = bf16[4,128,768]{2,1,0:T(8,128)(2,1)} all-to-all(bf16[4,128,768]{2,1,0:T(8,128)(2,1)S(1)} %bitcast.69), channel_id=1, replica_groups=mesh['groups'=2,'expert'=4,'tensor'=4] {'expert'}, dimensions={0} | all-to-all | bytes 1572864 | tf_op jit(solution)/shard_map/all_to_all | solution.py:58
  70.1 0.0 all-gather.3.cloned.1.call-update
  70.1 0.0 reduce-scatter.2.cloned.1.call-start
  70.2 5.0 %all-gather.5.cloned.1.call-done = bf16[4,128,3072]{2,1,0:T(8,128)(2,1)} async-done(((bf16[4,128,768]{2,1,0:T(8,128)(2,1)}), bf16[4,128,3072]{2,1,0:T(8,128)(2,1)}) %all-gather.5.cloned.1.call-update) | async-done | bytes 3145744 | tf_op jit(solution)/shard_map/all_gather | solution.py:60
  75.2 11.9 %fusion.2 = f32[512,2048]{1,0:T(8,128)} fusion(bf16[512,3072]{1,0:T(8,128)(2,1)} %bitcast.95, bf16[1,3072,2048]{2,1,0:T(8,128)(2,1)} %param.12), kind=kOutput, calls=%fused_computation.2 | convolution fusion | flops 6442450944 | bytes 19922944 | tf_op jit(solution)/shard_map/dot_general | solution.py:67
  87.1 18.3 %all-gather.3.cloned.1.call-done = bf16[4,128,3072]{2,1,0:T(8,128)(2,1)} async-done(((bf16[4,128,768]{2,1,0:T(8,128)(2,1)}), bf16[4,128,3072]{2,1,0:T(8,128)(2,1)}) %all-gather.3.cloned.1.call-update) | async-done | bytes 3145744 | tf_op jit(solution)/shard_map/all_gather | solution.py:62
  105.3 0.0 copy-start.6
  105.3 0.0 copy-start.7
  105.3 10.8 %fusion.8 = f32[512,2048]{1,0:T(8,128)S(1)} fusion(bf16[512,3072]{1,0:T(8,128)(2,1)} %bitcast.93, bf16[1,2048,3072]{2,1,0:T(8,128)(2,1)} %param.14), kind=kOutput, calls=%fused_computation.8 | convolution fusion | flops 6442450944 | bytes 19922944 | tf_op jit(solution)/shard_map/sd,fd->sf/dot_general | solution.py:74
  116.1 0.0 copy-done.6
  116.1 0.0 copy-done.7
  116.1 0.0 copy-start.8
  116.1 15.0 %add_reduce_fusion = (f32[512]{0:T(512)S(1)}, f32[512]{0:T(512)S(1)}, bf16[512,2048]{1,0:T(8,128)(2,1)S(1)}, f32[512,2048]{1,0:T(8,128)}) fusion(f32[512,2048]{1,0:T(8,128)S(1)} %copy-done.7, f32[512,2048]{1,0:T(8,128)S(1)} %fusion.8, bf16[512,3072]{1,0:T(8,128)(2,1)S(1)} %bitcast.96, bf16[1,3072,2048]{2,1,0:T(8,128)(2,1)} %param.13), kind=kOutput, calls=%fused_computation.14 | convolution fusion | flops 6468664320 | bytes 30412800 | tf_op jit(solution)/shard_map/dot_general | solution.py:68
  131.1 0.0 copy-done.8
  131.1 16.3 %fusion = f32[512,3072]{1,0:T(8,128)} fusion(bf16[1,3072,2048]{2,1,0:T(8,128)(2,1)} %param.12, f32[512,2048]{1,0:T(8,128)S(1)} %copy-done.7, f32[512,2048]{1,0:T(8,128)} %copy-done.8, f32[512,2048]{1,0:T(8,128)} %get-tuple-element.22), kind=kOutput, calls=%fused_computation | convolution fusion | flops 6452936704 | bytes 31457280 | tf_op jit(solution)/shard_map/sf,df->sd/dot_general | solution.py:79
  147.4 14.4 %add_convert_fusion = bf16[512,3072]{1,0:T(8,128)(2,1)} fusion(f32[512,3072]{1,0:T(8,128)} %fusion, bf16[1,3072,2048]{2,1,0:T(8,128)(2,1)} %param.13, f32[512,2048]{1,0:T(8,128)} %copy-done.8, f32[512,2048]{1,0:T(8,128)S(1)} %copy-done.7), kind=kOutput, calls=%fused_computation.11 | convolution fusion | flops 6451888128 | bytes 30408704 | tf_op jit(solution)/shard_map/sf,df->sd/dot_general | solution.py:80
  161.8 0.0 reduce-scatter.2.cloned.1.call-update
  161.8 0.1 fusion.27
  161.9 0.6 pad_maximum_fusion.1
  162.5 4.6 %all-to-all-start.3 = ((f32[2,4,128]{2,0,1:T(2,128)}), f32[2,4,128]{2,0,1:T(2,128)S(1)}, u32[]{:S(2)}, u32[]{:S(2)}) async-start(f32[2,4,128]{2,0,1:T(2,128)} %pad_maximum_fusion.1), calls=%async_computation.4 | async-start | bytes 8192 | tf_op jit(solution)/shard_map/all_to_all | solution.py:94
  167.1 0.0 copy-start.2
  167.1 0.0 copy-start.5
  167.2 0.0 copy-start.1
  167.2 11.7 %convert_bitcast_fusion = bf16[1,2048,3072]{2,1,0:T(8,128)(2,1)} fusion(bf16[512,2048]{1,0:T(8,128)(2,1)S(1)} %get-tuple-element.8, bf16[512,3072]{1,0:T(8,128)(2,1)} %bitcast.94), kind=kOutput, calls=%fused_computation.10 | convolution fusion | flops 6448742400 | bytes 17825792 | tf_op jit(solution)/shard_map/sf,sd->fd/dot_general | solution.py:71
  178.9 0.0 all-to-all-done.3
  178.9 0.7 fusion.12
  179.5 0.1 reshape.110
  179.7 6.6 %psum.30 = f32[2,2,192]{2,1,0:T(2,128)S(1)} all-reduce(f32[2,2,192]{2,1,0:T(2,128)S(1)} %reshape.110), channel_id=1, replica_groups=mesh['groups'=2,'expert'=4,'tensor'=4] {'tensor'}, use_global_device_ids=true, to_apply=%region_10.11 | all-reduce | flops 768 | bytes 6144 | tf_op jit(solution)/shard_map/psum | solution.py:98
  186.2 13.8 %reduce-scatter.2.cloned.1.call-done = bf16[512,768]{1,0:T(8,128)(2,1)} async-done(((bf16[512,3072]{1,0:T(8,128)(2,1)}), bf16[512,768]{1,0:T(8,128)(2,1)}) %reduce-scatter.2.cloned.1.call-update) | async-done | bytes 786448 | tf_op jit(solution)/shard_map/reduce_scatter | solution.py:87
  200.1 4.6 %all-to-all-start.2 = ((bf16[4,128,768]{2,1,0:T(8,128)(2,1)}), bf16[4,128,768]{2,1,0:T(8,128)(2,1)S(1)}, u32[]{:S(2)}, u32[]{:S(2)}) async-start(bf16[4,128,768]{2,1,0:T(8,128)(2,1)} %bitcast.67), calls=%async_computation.3 | async-start | bytes 1572864 | tf_op jit(solution)/shard_map/all_to_all | solution.py:90
  204.8 0.0 copy-done.2
  204.8 0.0 copy-done.5
  204.8 0.5 fusion.18
  205.3 0.0 copy-done.3
  205.3 0.7 fusion.47
  206.0 18.8 %all-to-all-done.2 = bf16[4,128,768]{2,1,0:T(8,128)(2,1)S(1)} async-done(((bf16[4,128,768]{2,1,0:T(8,128)(2,1)}), bf16[4,128,768]{2,1,0:T(8,128)(2,1)S(1)}, u32[]{:S(2)}, u32[]{:S(2)}) %all-to-all-start.2) | async-done | bytes 786464 | tf_op jit(solution)/shard_map/all_to_all | solution.py:90
  224.8 1.2 fusion.26
  226.0 17.1 %psum.31 = f32[5,768]{1,0:T(8,128)S(1)} all-reduce(f32[5,768]{1,0:T(8,128)S(1)} %pad_maximum_fusion), channel_id=1, replica_groups=mesh['groups'=2,'expert'=4,'tensor'=4] {'expert'}, use_global_device_ids=true, to_apply=%region_13.14 | all-reduce | flops 3840 | bytes 30720 | tf_op jit(solution)/shard_map/psum | solution.py:117
  243.1 0.6 slice_reduce_fusion.1
  243.7 0.6 slice_bitcast_fusion
  244.3 0.0 copy-done.1
  (15 shorter events, 0.2 us)
Async XLA Ops:
  7.2 40.3 %copy-start = (bf16[192,768]{1,0:T(8,128)(2,1)S(1)}, bf16[192,768]{1,0:T(8,128)(2,1)}, u32[]{:S(2)}) copy-start(bf16[192,768]{1,0:T(8,128)(2,1)} %param.15) | copy-start | bytes 884740
  7.2 40.2 %copy-start.4 = (s32[192,2]{0,1:T(2,128)S(1)}, s32[192,2]{0,1:T(2,128)}, u32[]{:S(2)}) copy-start(s32[192,2]{0,1:T(2,128)} %param.11) | copy-start | bytes 4612
  7.2 68.0 %all-gather.5.cloned.1.call-start = ((), (), s32[]{:S(2)}) async-start(), calls=%async_computation.6 | async-start | bytes 3932160 | tf_op jit(solution)/shard_map/all_gather | solution.py:60
  47.3 58.0 %all-gather.3.cloned.1.call-start = ((), (), s32[]{:S(2)}) async-start(), calls=%async_computation.5 | async-start | bytes 3932160 | tf_op jit(solution)/shard_map/all_gather | solution.py:62
  70.1 129.9 %reduce-scatter.2.cloned.1.call-start = ((), (), s32[]{:S(2)}) async-start(), calls=%async_computation.7 | async-start | bytes 3932160 | tf_op jit(solution)/shard_map/reduce_scatter | solution.py:87
  105.3 10.8 %copy-start.6 = (bf16[4,128,3072]{2,1,0:T(8,128)(2,1)S(1)}, bf16[4,128,3072]{2,1,0:T(8,128)(2,1)}, u32[]{:S(2)}) copy-start(bf16[4,128,3072]{2,1,0:T(8,128)(2,1)} %all-gather.5.cloned.1.call-done) | copy-start | bytes 9437188
  105.3 10.8 %copy-start.7 = (f32[512,2048]{1,0:T(8,128)S(1)}, f32[512,2048]{1,0:T(8,128)}, u32[]{:S(2)}) copy-start(f32[512,2048]{1,0:T(8,128)} %fusion.2) | copy-start | bytes 12582916
  116.1 15.0 %copy-start.8 = (f32[512,2048]{1,0:T(8,128)}, f32[512,2048]{1,0:T(8,128)S(1)}, u32[]{:S(2)}) copy-start(f32[512,2048]{1,0:T(8,128)S(1)} %fusion.8) | copy-start | bytes 12582916
  162.5 16.3 %all-to-all-start.3 = ((f32[2,4,128]{2,0,1:T(2,128)}), f32[2,4,128]{2,0,1:T(2,128)S(1)}, u32[]{:S(2)}, u32[]{:S(2)}) async-start(f32[2,4,128]{2,0,1:T(2,128)} %pad_maximum_fusion.1), calls=%async_computation.4 | async-start | bytes 8192 | tf_op jit(solution)/shard_map/all_to_all | solution.py:94
  167.1 37.6 %copy-start.2 = (bf16[192,768]{1,0:T(8,128)(2,1)S(1)}, bf16[192,768]{1,0:T(8,128)(2,1)}, u32[]{:S(2)}) copy-start(bf16[192,768]{1,0:T(8,128)(2,1)} %param.8) | copy-start | bytes 884740
  167.1 37.6 %copy-start.5 = (f32[768]{0:T(1024)S(1)}, f32[768]{0:T(1024)}, u32[]{:S(2)}) copy-start(f32[768]{0:T(1024)} %param.9) | copy-start | bytes 9220
  167.1 38.1 %copy-start.3 = (f32[768,4]{0,1:T(4,128)S(1)}, f32[768,4]{0,1:T(4,128)}, u32[]{:S(2)}) copy-start(f32[768,4]{0,1:T(4,128)} %param.10) | copy-start | bytes 36868
  167.2 77.2 %copy-start.1 = (bf16[192,768]{1,0:T(8,128)(2,1)S(1)}, bf16[192,768]{1,0:T(8,128)(2,1)}, u32[]{:S(2)}) copy-start(bf16[192,768]{1,0:T(8,128)(2,1)} %param.15) | copy-start | bytes 884740
  200.1 24.7 %all-to-all-start.2 = ((bf16[4,128,768]{2,1,0:T(8,128)(2,1)}), bf16[4,128,768]{2,1,0:T(8,128)(2,1)S(1)}, u32[]{:S(2)}, u32[]{:S(2)}) async-start(bf16[4,128,768]{2,1,0:T(8,128)(2,1)} %bitcast.67), calls=%async_computation.3 | async-start | bytes 1572864 | tf_op jit(solution)/shard_map/all_to_all | solution.py:90
Sparse Core Ops, SparseCore 0:
  47.4 27.7 all-gather.4
  76.8 28.5 all-gather.2
  161.9 38.0 reduce-scatter.1

commit v2 on v1

--- a/solution.py
+++ b/solution.py
@@ -1,10 +1,266 @@
 import jax
 import jax.numpy as jnp
 from jax import lax
+from jax.experimental import pallas as pl
+from jax.experimental.pallas import tpu as pltpu
 from jax.sharding import PartitionSpec as P
 
 EPS = 1e-05
 PRECISE = lax.Precision.HIGHEST
+
+
+def meet(peers):
+    barrier = pltpu.get_barrier_semaphore()
+    for peer in peers:
+        pl.semaphore_signal(barrier, inc=1, device_id=peer, device_id_type=pl.DeviceIdType.MESH)
+    pl.semaphore_wait(barrier, len(peers))
+
+
+def remote(src, dst, send, recv, peer):
+    return pltpu.make_async_remote_copy(
+        src_ref=src,
+        dst_ref=dst,
+        send_sem=send,
+        recv_sem=recv,
+        device_id=peer,
+        device_id_type=pl.DeviceIdType.MESH,
+    )
+
+
+def small_psum(part, axis, collective_id):
+    count = lax.axis_size(axis)
+
+    def kernel(part_ref, out_ref, land, send, recv):
+        me = lax.axis_index(axis)
+        peers = [{axis: lax.rem(me + k, count)} for k in range(1, count)]
+        meet(peers)
+        copies = [
+            remote(part_ref, land.at[me], send.at[k], recv.at[k], peer)
+            for k, peer in enumerate(peers)
+        ]
+        for copy in copies:
+            copy.start()
+        land[me] = part_ref[...]
+        for copy in copies:
+            copy.wait_recv()
+        total = land[0]
+        for source in range(1, count):
+            total = total + land[source]
+        out_ref[...] = total
+        for copy in copies:
+            copy.wait_send()
+
+    return pl.pallas_call(
+        kernel,
+        out_shape=jax.ShapeDtypeStruct(part.shape, part.dtype),
+        in_specs=[pl.BlockSpec(memory_space=pltpu.VMEM)],
+        out_specs=pl.BlockSpec(memory_space=pltpu.VMEM),
+        scratch_shapes=[
+            pltpu.VMEM((count,) + part.shape, part.dtype),
+            pltpu.SemaphoreType.DMA((count - 1,)),
+            pltpu.SemaphoreType.DMA((count - 1,)),
+        ],
+        compiler_params=pltpu.CompilerParams(collective_id=collective_id, has_side_effects=True),
+    )(part)
+
+
+def gather_slots(send_grads, send_rows):
+    experts, capacity, cols = send_rows.shape
+    slots = experts * capacity
+
+    def kernel(
+        grads_ref, rows_ref, out_grads, out_rows,
+        own_sem, z_send, z_recv, x_send, x_recv, m_send, m_recv, n_send, n_recv,
+    ):
+        z = lax.axis_index("expert")
+        t = lax.axis_index("tensor")
+        over_x = {"tensor": lax.rem(t + 2, 4)}
+        mate = {"tensor": t + 1 - 2 * lax.rem(t, 2)}
+        zs = [lax.rem(z + k, experts) for k in range(experts)]
+        from_z = [lax.rem(z + experts - k, experts) for k in range(experts)]
+        outs = (out_grads, out_rows)
+        ins = (grads_ref, rows_ref)
+        meet([over_x, mate] + [{"expert": zd} for zd in zs[1:]])
+
+        def block(a, source, quarter):
+            return outs[a].at[
+                pl.ds(pl.multiple_of(source * capacity, capacity), capacity),
+                pl.ds(pl.multiple_of(quarter * cols, 128), cols),
+            ]
+
+        z_copies = {}
+        for a in range(2):
+            for k in (2, 3, 1)[: experts - 1]:
+                copy = remote(
+                    ins[a].at[zs[k]], block(a, z, t), z_send.at[a, k], z_recv.at[a, k],
+                    {"expert": zs[k]},
+                )
+                copy.start()
+                z_copies[a, k] = copy
+        x_copies, m_copies, n_copies = {}, {}, {}
+        quarter_x = lax.rem(t + 2, 4)
+        order = [(a, k) for a in range(2) for k in (0, 1, 3, 2)]
+
+        def pass_on(a, k):
+            far = block(a, from_z[k], quarter_x)
+            x_copies[a, k].wait_recv()
+            n_copies[a, k] = remote(far, far, n_send.at[a, k], n_recv.at[a, k], mate)
+            n_copies[a, k].start()
+
+        for i, (a, k) in enumerate(order):
+            near = block(a, from_z[k], t)
+            if k == 0:
+                own = pltpu.make_async_copy(ins[a].at[z], near, own_sem.at[a])
+                own.start()
+                own.wait()
+            else:
+                z_copies[a, k].wait_recv()
+            x_copies[a, k] = remote(near, near, x_send.at[a, k], x_recv.at[a, k], over_x)
+            x_copies[a, k].start()
+            m_copies[a, k] = remote(near, near, m_send.at[a, k], m_recv.at[a, k], mate)
+            m_copies[a, k].start()
+            if i:
+                pass_on(*order[i - 1])
+        pass_on(*order[-1])
+        for group in (m_copies, n_copies):
+            for copy in group.values():
+                copy.wait_recv()
+        for group in (z_copies, x_copies, m_copies, n_copies):
+            for copy in group.values():
+                copy.wait_send()
+
+    sems = [pltpu.SemaphoreType.DMA((2, experts)) for _ in range(8)]
+    shape = jax.ShapeDtypeStruct((slots, 4 * cols), send_rows.dtype)
+    return pl.pallas_call(
+        kernel,
+        out_shape=(shape, shape),
+        in_specs=[pl.BlockSpec(memory_space=pltpu.VMEM)] * 2,
+        out_specs=[pl.BlockSpec(memory_space=pltpu.VMEM)] * 2,
+        scratch_shapes=[pltpu.SemaphoreType.DMA((2,))] + sems,
+        compiler_params=pltpu.CompilerParams(
+            collective_id=2, has_side_effects=True, vmem_limit_bytes=24 * 1024 * 1024
+        ),
+    )(send_grads, send_rows)
+
+
+def return_slots(row_part, scalars, experts, capacity, cols):
+    def kernel(
+        part_ref, scal_ref, out_rows, out_scal,
+        m_land, x_out, kept, x_land, z_out, s_land, s_x, s_xland, s_z,
+        m_send, m_recv, x_send, x_recv, z_send, z_recv,
+        sm_send, sm_recv, sx_send, sx_recv, sz_send, sz_recv,
+    ):
+        z = lax.axis_index("expert")
+        t = lax.axis_index("tensor")
+        x_mine = t // 2
+        core = lax.rem(t, 2)
+        over_x = {"tensor": lax.rem(t + 2, 4)}
+        mate = {"tensor": t + 1 - 2 * core}
+        zs = [lax.rem(z + k, experts) for k in range(experts)]
+        order = (2, 3, 1, 0)
+        meet([over_x, mate] + [{"expert": zd} for zd in zs[1:]])
+
+        def rows(k):
+            return pl.ds(pl.multiple_of(zs[k] * capacity, capacity), capacity)
+
+        def lanes(quarter):
+            return pl.ds(pl.multiple_of(quarter * cols, 128), cols)
+
+        pending = []
+        s_m = remote(scal_ref, s_land, sm_send, sm_recv, mate)
+        m_copies = {}
+        for n, k in enumerate(order):
+            for j in range(2):
+                xq = lax.rem(x_mine + 1 + j, 2)
+                m_copies[k, j] = remote(
+                    part_ref.at[rows(k), lanes(2 * xq + 1 - core)],
+                    m_land.at[k, j], m_send.at[k, j], m_recv.at[k, j], mate,
+                )
+                m_copies[k, j].start()
+            if n == 0:
+                s_m.start()
+        pending += list(m_copies.values()) + [s_m]
+        x_copies, z_copies = {}, {}
+        quarter_x = lax.rem(t + 2, 4)
+
+        def finish(k):
+            x_copies[k].wait_recv()
+            z_out[k] = (kept[k] + x_land[k].astype(jnp.float32)).astype(jnp.bfloat16)
+            if k:
+                z_copies[k] = remote(
+                    z_out.at[k], out_rows.at[z], z_send.at[k], z_recv.at[k], {"expert": zs[k]}
+                )
+                z_copies[k].start()
+            else:
+                out_rows[z] = z_out[0]
+
+        for n, k in enumerate(order):
+            m_copies[k, 0].wait_recv()
+            x_out[k] = (
+                part_ref[rows(k), lanes(quarter_x)].astype(jnp.float32)
+                + m_land[k, 0].astype(jnp.float32)
+            ).astype(jnp.bfloat16)
+            x_copies[k] = remote(x_out.at[k], x_land.at[k], x_send.at[k], x_recv.at[k], over_x)
+            x_copies[k].start()
+            if n == 0:
+                s_m.wait_recv()
+                s_x[...] = scal_ref[...] + s_land[...]
+                s_xc = remote(s_x, s_xland, sx_send, sx_recv, over_x)
+                s_xc.start()
+                pending.append(s_xc)
+            m_copies[k, 1].wait_recv()
+            kept[k] = part_ref[rows(k), lanes(t)].astype(jnp.float32) + m_land[k, 1].astype(
+                jnp.float32
+            )
+            if n:
+                finish(order[n - 1])
+            if n == 1:
+                s_xc.wait_recv()
+                s_z[...] = s_x[...] + s_xland[...]
+                for j in range(1, experts):
+                    copy = remote(
+                        s_z.at[zs[j]], out_scal.at[z], sz_send.at[j], sz_recv.at[j],
+                        {"expert": zs[j]},
+                    )
+                    copy.start()
+                    z_copies["s", j] = copy
+                out_scal[z] = s_z[z]
+        finish(order[-1])
+        for copy in z_copies.values():
+            copy.wait_recv()
+        for copy in pending + list(x_copies.values()) + list(z_copies.values()):
+            copy.wait_send()
+
+    f32, bf16, dma = jnp.float32, jnp.bfloat16, pltpu.SemaphoreType.DMA
+    chunk = (experts, capacity, cols)
+    return pl.pallas_call(
+        kernel,
+        out_shape=(
+            jax.ShapeDtypeStruct(chunk, bf16),
+            jax.ShapeDtypeStruct(scalars.shape, f32),
+        ),
+        in_specs=[pl.BlockSpec(memory_space=pltpu.VMEM)] * 2,
+        out_specs=[pl.BlockSpec(memory_space=pltpu.VMEM)] * 2,
+        scratch_shapes=[
+            pltpu.VMEM((experts, 2, capacity, cols), bf16),
+            pltpu.VMEM(chunk, bf16),
+            pltpu.VMEM(chunk, f32),
+            pltpu.VMEM(chunk, bf16),
+            pltpu.VMEM(chunk, bf16),
+            pltpu.VMEM(scalars.shape, f32),
+            pltpu.VMEM(scalars.shape, f32),
+            pltpu.VMEM(scalars.shape, f32),
+            pltpu.VMEM(scalars.shape, f32),
+            dma((experts, 2)), dma((experts, 2)),
+            dma((experts,)), dma((experts,)),
+            dma((experts,)), dma((experts,)),
+            dma, dma, dma, dma,
+            dma((experts,)), dma((experts,)),
+        ],
+        compiler_params=pltpu.CompilerParams(
+            collective_id=3, has_side_effects=True, vmem_limit_bytes=32 * 1024 * 1024
+        ),
+    )(row_part, scalars)
 
 
 def body(
@@ -14,11 +270,19 @@
     expert_count = router_weight.shape[1]
     feat_width = part_cols * lax.axis_size("tensor")
     capacity = 8 * tok_rows // (3 * expert_count)
+    direct = lax.axis_size("tensor") == 4 and expert_count == 4 and part_cols % 128 == 0
     inputs_f = hidden_in.astype(jnp.float32)
     scaled_in = inputs_f * norm_gain[None, :]
     square_part = jnp.sum(inputs_f * inputs_f, axis=1)
-    logit_part = jnp.dot(scaled_in, router_weight, precision=PRECISE)
-    square_sum, logit_sum = lax.psum((square_part, logit_part), "tensor")
+    logit_part = jnp.einsum("td,de->et", scaled_in, router_weight, precision=PRECISE)
+    token_part = jnp.concatenate([square_part[None, :], logit_part], axis=0)
+    if direct:
+        padding = ((0, -token_part.shape[0] % 8), (0, -tok_rows % 128))
+        token_sum = small_psum(jnp.pad(token_part, padding), "tensor", 0)
+    else:
+        token_sum = lax.psum(token_part, "tensor")
+    square_sum = token_sum[0, :tok_rows]
+    logit_sum = token_sum[1 : 1 + expert_count, :tok_rows].T
     inv_rms = lax.rsqrt(square_sum / feat_width + EPS)[:, None]
     normed = scaled_in * inv_rms
     normed_b = normed.astype(jnp.bfloat16)
@@ -54,13 +318,16 @@
 
     send_grads = dispatch(pick_weight, grad_out)
     send_rows = dispatch(pick_bf, normed_b)
-    got_rows = lax.all_to_all(send_rows, "expert", split_axis=0, concat_axis=0, tiled=True)
-    got_grads = lax.all_to_all(send_grads, "expert", split_axis=0, concat_axis=0, tiled=True)
-    slot_total = got_rows.shape[0] * capacity
-    slot_rows = lax.all_gather(got_rows, "tensor", axis=2, tiled=True)
-    slot_rows = slot_rows.reshape(slot_total, feat_width)
-    out_grad = lax.all_gather(got_grads, "tensor", axis=2, tiled=True)
-    out_grad = out_grad.reshape(slot_total, feat_width)
+    slot_total = expert_count * capacity
+    if direct:
+        out_grad, slot_rows = gather_slots(send_grads, send_rows)
+    else:
+        got_rows = lax.all_to_all(send_rows, "expert", split_axis=0, concat_axis=0, tiled=True)
+        got_grads = lax.all_to_all(send_grads, "expert", split_axis=0, concat_axis=0, tiled=True)
+        slot_rows = lax.all_gather(got_rows, "tensor", axis=2, tiled=True)
+        slot_rows = slot_rows.reshape(slot_total, feat_width)
+        out_grad = lax.all_gather(got_grads, "tensor", axis=2, tiled=True)
+        out_grad = out_grad.reshape(slot_total, feat_width)
     gate_matrix = gate_weight[0]
     up_matrix = up_weight[0]
     down_matrix = down_weight[0]
@@ -84,18 +351,28 @@
     inner_part = jnp.sum(
         gate_grad.astype(jnp.float32) * gate_pre + up_grad.astype(jnp.float32) * up_pre, axis=1
     )
-    row_own = lax.psum_scatter(
-        row_part.astype(jnp.bfloat16), "tensor", scatter_dimension=1, tiled=True
-    )
-    back_rows = lax.all_to_all(
-        row_own.reshape(-1, capacity, part_cols), "expert", split_axis=0, concat_axis=0, tiled=True
-    ).reshape(expert_count * capacity, part_cols)
-    scalars = jnp.stack([inner_part, prob_part], axis=0).reshape(2, -1, capacity)
-    scalars = lax.all_to_all(scalars, "expert", split_axis=1, concat_axis=1, tiled=True)
-    scalars = scalars.reshape(2, expert_count * capacity)
+    row_part = row_part.astype(jnp.bfloat16)
+    if direct:
+        scalars = jnp.stack([inner_part, prob_part], axis=0).reshape(2, expert_count, capacity)
+        scalars = jnp.pad(scalars.transpose(1, 0, 2), ((0, 0), (0, 6), (0, 0)))
+        back_rows, scalars = return_slots(row_part, scalars, expert_count, capacity, part_cols)
+        back_rows = back_rows.reshape(slot_total, part_cols)
+        scalars = scalars[:, :2].transpose(1, 0, 2).reshape(2, slot_total)
+    else:
+        row_own = lax.psum_scatter(
+            row_part, "tensor", scatter_dimension=1, tiled=True
+        )
+        back_rows = lax.all_to_all(
+            row_own.reshape(-1, capacity, part_cols), "expert", split_axis=0, concat_axis=0, tiled=True
+        ).reshape(expert_count * capacity, part_cols)
+        scalars = jnp.stack([inner_part, prob_part], axis=0).reshape(2, -1, capacity)
+        scalars = lax.all_to_all(scalars, "expert", split_axis=1, concat_axis=1, tiled=True)
+        scalars = scalars.reshape(2, expert_count * capacity)
     pick_token = jnp.concatenate([pick_first, pick_second], axis=0)
     token_scalars = jnp.einsum("cs,ts->ct", scalars, pick_token, precision=PRECISE)
-    token_scalars = lax.psum(token_scalars, "tensor").reshape(2, 2, tok_rows)
+    if not direct:
+        token_scalars = lax.psum(token_scalars, "tensor")
+    token_scalars = token_scalars.reshape(2, 2, tok_rows)
     expert_grad = jnp.dot(pick_bf, back_rows, preferred_element_type=jnp.float32)
     token_inner = token_scalars[0, 0] + token_scalars[0, 1]
     ratio_first = prob_first / jnp.where(prob_first_b == 0, 1, prob_first_b).astype(jnp.float32)
@@ -114,7 +391,12 @@
     ).astype(jnp.bfloat16)
     gain_part = jnp.sum(total_grad * inputs_f * inv_rms, axis=0)
     router_part = jnp.einsum("td,te->de", normed, logit_grad, precision=PRECISE)
-    sums = lax.psum(jnp.concatenate([gain_part[None, :], router_part.T], axis=0), "expert")
+    sums = jnp.concatenate([gain_part[None, :], router_part.T], axis=0)
+    if direct:
+        sums = small_psum(jnp.pad(sums, ((0, -sums.shape[0] % 8), (0, 0))), "expert", 1)
+        sums = sums[: 1 + expert_count]
+    else:
+        sums = lax.psum(sums, "expert")
     grad_gain, grad_router = sums[0], sums[1:].T
     return (grad_input, grad_gain, grad_router, grad_down)
 

time: 251 us -> 201 us (0.80)
  Pallas kernels: 0 us -> 104 us
  blocking collectives: 77.8 us -> 0 us
  waiting for transfers between devices: 56 us -> 0 us
  between operations: 14 us -> 0.92 us
  starting transfers between devices: 9.34 us -> 0 us
  matrix products: 86.6 us -> 84 us
    pallas_call x0 -> x4, Pallas kernels: none -> 104 us  [the longest x1 51.2 us: gather_slots(): pl.pallas_call(kernel, out_shape=(shape, shape), in_specs=[pl.BlockSpec(m...]
    all_to_all x2 -> x0, blocking collectives: 45.7 us -> none  [the longest x1 23.6 us: body(): lax.all_to_all(send_rows, 'expert', split_axis=0, concat_axis=0, tiled=True)]
    psum x3 -> x0, blocking collectives: 32.1 us -> none  [the longest x1 17.1 us: body(): lax.psum(jnp.concatenate([gain_part[None, :], router_part.T], axis=0), 'e...]
    all_gather x2 -> x0, waiting for transfers between devices: 23.3 us -> none  [the longest x1 18.3 us: body(): out_grad = lax.all_gather(got_grads, 'tensor', axis=2, tiled=True)]
    all_to_all x2 -> x0, waiting for transfers between devices: 18.8 us -> none  [the longest x1 18.8 us: body(): lax.all_to_all(row_own.reshape(-1, capacity, part_cols), 'expert', split_...]
    reduce_scatter x1 -> x0, waiting for transfers between devices: 13.8 us -> none  [body(): lax.psum_scatter(row_part.astype(jnp.bfloat16), 'tensor', scatter_dimensi...]
    all_to_all x2 -> x0, starting transfers between devices: 9.22 us -> none  [the longest x1 4.62 us: body(): lax.all_to_all(row_own.reshape(-1, capacity, part_cols), 'expert', split_...]
  transfers between devices with their start and end apart: 5 -> 0, of which waited for: 4 -> 0; matrix products, arithmetic and copies ran while one was open for 11% -> 0% of each run, Pallas kernels for 0% -> 0%
where the time goes in v2:
time: 201 us; the launch traced here: 200 us
  Pallas kernels  104 us (52%)
  matrix products  84 us (42%)
  other arithmetic  6.26 us (3%)
  local copies, waits for them, and re-layouts  5.04 us (3%)
    pallas_call x1, Pallas kernels, gather_slots(): pl.pallas_call(kernel, out_shape=(shape, shape), in_specs=[pl.BlockSpec(m...  51.2 us
    pallas_call x1, Pallas kernels, return_slots(): pl.pallas_call(kernel, out_shape=(jax.ShapeDtypeStruct(chunk, bf16), jax....  39.9 us
    dot_general x1, matrix products, body(): jnp.einsum('sf,df->sd', gate_grad, gate_matrix, preferred_element_type=jn...  17.5 us
    dot_general x1, matrix products, body(): up_pre = jnp.dot(slot_rows, up_matrix, preferred_element_type=jnp.float32)  16.6 us
    dot_general x1, matrix products, body(): jnp.einsum('sf,df->sd', up_grad, up_matrix, preferred_element_type=jnp.fl...  13.1 us
    pallas_call x2, Pallas kernels, small_psum(): pl.pallas_call(kernel, out_shape=jax.ShapeDtypeStruct(part.shape, part.dt...  13 us
    dot_general x1, matrix products, body(): jnp.einsum('sf,sd->fd', hidden_act, out_grad, preferred_element_type=jnp....  11.3 us
    dot_general x1, matrix products, body(): jnp.dot(slot_rows, gate_matrix, preferred_element_type=jnp.float32)  11.2 us

profile of v2, /device:TPU:0, one launch (start us, length us, event | category | flops | bytes accessed | tf_op | source)
XLA Modules:
  0.0 200.3 jit_solution(17677175247376442321)
XLA Ops:
  0.6 0.0 copy-start
  0.6 0.0 copy-start.2
  0.7 0.0 copy-start.6
  0.7 1.6 convolution_bitcast_fusion
  2.3 1.1 fusion.16
  3.4 0.6 select_maximum_fusion.1.part_ref
  4.0 5.9 %shard_map.111 = f32[8,256]{1,0:T(8,128)} custom-call(f32[8,256]{1,0:T(8,128)} %select_maximum_fusion.1.part_ref), custom_call_target="tpu_custom_call" | custom-call | tf_op jit(solution)/shard_map/pallas_call | solution.py:53
  9.9 0.7 fusion.57
  10.6 0.8 copy.20
  11.4 0.1 eq.103
  11.6 1.2 reduce-window.6
  12.8 0.2 slice_reduce_fusion
  13.0 0.2 reduce-window.9
  13.2 0.1 add_bitcast_fusion
  13.3 0.1 eq.99
  13.5 0.1 reduce_sum.67
  13.6 0.1 copy.22
  13.7 0.7 multiply_add_fusion
  14.4 0.1 fusion.22
  14.5 0.1 pad_maximum_fusion
  14.6 0.8 fusion.60
  15.3 0.7 fusion.41
  16.1 0.0 copy-done
  16.1 0.5 convolution_convert_fusion.1
  16.6 0.0 copy-done.2
  16.7 0.0 copy-done.6
  16.7 0.5 convolution_convert_fusion
  17.2 0.0 slice-start
  17.2 51.2 %shard_map.112 = (bf16[512,3072]{1,0:T(8,128)(2,1)S(1)}, bf16[512,3072]{1,0:T(8,128)(2,1)S(1)}) custom-call(bf16[4,128,768]{2,1,0:T(8,128)(2,1)S(1)} %bitcast.84, bf16[4,128,768]{2,1,0:T(8,128)(2,1)S(1)} %bitcast.85), custom_call_target="tpu_custom_call" | custom-call | tf_op jit(solution)/shard_map/pallas_call | solution.py:134
  68.4 0.0 slice-start.1
  68.4 0.0 slice-start.2
  68.4 11.2 %fusion.2 = f32[512,2048]{1,0:T(8,128)} fusion(bf16[512,3072]{1,0:T(8,128)(2,1)S(1)} %get-tuple-element.9, bf16[1,3072,2048]{2,1,0:T(8,128)(2,1)} %param.12), kind=kOutput, calls=%fused_computation.2 | convolution fusion | flops 6442450944 | bytes 19922944 | tf_op jit(solution)/shard_map/dot_general | solution.py:334
  79.7 0.0 slice-done
  79.7 0.0 slice-done.1
  79.7 0.0 slice-done.2
  79.7 8.6 %fusion.8 = f32[512,2048]{1,0:T(8,128)} fusion(bf16[512,3072]{1,0:T(8,128)(2,1)S(1)} %get-tuple-element.8, bf16[1,2048,3072]{2,1,0:T(8,128)(2,1)S(1)} %bitcast.119), kind=kOutput, calls=%fused_computation.8 | convolution fusion | flops 6442450944 | bytes 19922944 | tf_op jit(solution)/shard_map/sd,fd->sf/dot_general | solution.py:341
  88.3 16.6 %add_reduce_fusion = (f32[512]{0:T(512)S(1)}, f32[512]{0:T(512)S(1)}, bf16[512,2048]{1,0:T(8,128)(2,1)}, f32[512,2048]{1,0:T(8,128)}) fusion(f32[512,2048]{1,0:T(8,128)} %fusion.2, f32[512,2048]{1,0:T(8,128)} %fusion.8, bf16[512,3072]{1,0:T(8,128)(2,1)S(1)} %get-tuple-element.9, bf16[1,3072,2048]{2,1,0:T(8,128)(2,1)} %param.13), kind=kOutput, calls=%fused_computation.14 | convolution fusion | flops 6468664320 | bytes 30412800 | tf_op jit(solution)/shard_map/dot_general | solution.py:335
  104.9 17.5 %fusion = f32[512,3072]{1,0:T(8,128)} fusion(bf16[1,3072,2048]{2,1,0:T(8,128)(2,1)} %param.12, f32[512,2048]{1,0:T(8,128)} %fusion.2, f32[512,2048]{1,0:T(8,128)} %fusion.8, f32[512,2048]{1,0:T(8,128)} %get-tuple-element.28), kind=kOutput, calls=%fused_computation | convolution fusion | flops 6452936704 | bytes 31457280 | tf_op jit(solution)/shard_map/sf,df->sd/dot_general | solution.py:346
  122.3 0.0 copy-start.5
  122.3 0.0 copy-start.4
  122.3 13.1 %add_convert_fusion.part_ref = bf16[512,3072]{1,0:T(8,128)(2,1)S(1)} fusion(f32[512,3072]{1,0:T(8,128)} %fusion, bf16[1,3072,2048]{2,1,0:T(8,128)(2,1)} %param.13, f32[512,2048]{1,0:T(8,128)} %fusion.8, f32[512,2048]{1,0:T(8,128)} %fusion.2), kind=kOutput, calls=%fused_computation.11 | convolution fusion | flops 6451888128 | bytes 30408704 | tf_op jit(solution)/shard_map/sf,df->sd/dot_general | solution.py:347
  135.4 0.0 copy-start.3
  135.5 39.9 %shard_map.113 = (bf16[4,128,768]{2,1,0:T(8,128)(2,1)S(1)}, f32[4,8,128]{2,1,0:T(8,128)S(1)}) custom-call(bf16[512,3072]{1,0:T(8,128)(2,1)S(1)} %add_convert_fusion.part_ref, f32[4,8,128]{2,1,0:T(8,128)S(1)} %pad.13.scal_ref), custom_call_target="tpu_custom_call" | custom-call | tf_op jit(solution)/shard_map/pallas_call | solution.py:236
  175.3 0.7 fusion.39
  176.1 0.0 copy-done.5
  176.2 0.0 copy-done.4
  176.2 0.7 fusion.46
  176.9 0.0 copy-done.3
  176.9 1.2 fusion.21
  178.1 0.5 fusion.13
  178.6 0.6 select_maximum_fusion.part_ref
  179.2 7.1 %shard_map.114 = f32[8,768]{1,0:T(8,128)} custom-call(f32[8,768]{1,0:T(8,128)} %select_maximum_fusion.part_ref), custom_call_target="tpu_custom_call" | custom-call | tf_op jit(solution)/shard_map/pallas_call | solution.py:53
  186.3 1.3 slice_reduce_fusion.1
  187.6 1.3 slice_bitcast_fusion
  189.0 0.0 copy-start.1
  189.0 11.3 %convert_bitcast_fusion = bf16[1,2048,3072]{2,1,0:T(8,128)(2,1)} fusion(bf16[512,2048]{1,0:T(8,128)(2,1)} %get-tuple-element.14, bf16[512,3072]{1,0:T(8,128)(2,1)S(1)} %get-tuple-element.8), kind=kOutput, calls=%fused_computation.10 | convolution fusion | flops 6448742400 | bytes 17825792 | tf_op jit(solution)/shard_map/sf,sd->fd/dot_general | solution.py:338
  200.3 0.0 copy-done.1
  (14 shorter events, 0.1 us)
Async XLA Ops:
  0.6 15.5 %copy-start = (bf16[192,768]{1,0:T(8,128)(2,1)S(1)}, bf16[192,768]{1,0:T(8,128)(2,1)}, u32[]{:S(2)}) copy-start(bf16[192,768]{1,0:T(8,128)(2,1)} %param.15) | copy-start | bytes 884740
  0.6 16.0 %copy-start.2 = (bf16[192,768]{1,0:T(8,128)(2,1)S(1)}, bf16[192,768]{1,0:T(8,128)(2,1)}, u32[]{:S(2)}) copy-start(bf16[192,768]{1,0:T(8,128)(2,1)} %param.8) | copy-start | bytes 884740
  0.7 16.0 %copy-start.6 = (f32[768]{0:T(1024)S(1)}, f32[768]{0:T(1024)}, u32[]{:S(2)}) copy-start(f32[768]{0:T(1024)} %param.9) | copy-start | bytes 9220
  17.2 62.5 %slice-start = ((s8[12582912]{0:T(1024)(128)(4,1)}), s8[4194304]{0:T(1024)(128)(4,1)S(1)}, s32[]{:S(2)}) async-start(s8[12582912]{0:T(1024)(128)(4,1)} %bitcast.118), calls=%async_computation | async-start | bytes 8388608
  68.4 11.2 %slice-start.1 = ((s8[12582912]{0:T(1024)(128)(4,1)}), s8[4194304]{0:T(1024)(128)(4,1)S(1)}, s32[]{:S(2)}) async-start(s8[12582912]{0:T(1024)(128)(4,1)} %bitcast.118), calls=%async_computation.1 | async-start | bytes 8388608
  68.4 11.2 %slice-start.2 = ((s8[12582912]{0:T(1024)(128)(4,1)}), s8[4194304]{0:T(1024)(128)(4,1)S(1)}, s32[]{:S(2)}) async-start(s8[12582912]{0:T(1024)(128)(4,1)} %bitcast.118), calls=%async_computation.2 | async-start | bytes 8388608
  122.3 53.8 %copy-start.5 = (f32[8,256]{1,0:T(8,128)S(1)}, f32[8,256]{1,0:T(8,128)}, u32[]{:S(2)}) copy-start(f32[8,256]{1,0:T(8,128)} %shard_map.111) | copy-start | bytes 24580
  122.3 53.9 %copy-start.4 = (f32[768,4]{0,1:T(4,128)S(1)}, f32[768,4]{0,1:T(4,128)}, u32[]{:S(2)}) copy-start(f32[768,4]{0,1:T(4,128)} %param.10) | copy-start | bytes 36868
  135.4 41.5 %copy-start.3 = (bf16[192,768]{1,0:T(8,128)(2,1)S(1)}, bf16[192,768]{1,0:T(8,128)(2,1)}, u32[]{:S(2)}) copy-start(bf16[192,768]{1,0:T(8,128)(2,1)} %param.8) | copy-start | bytes 884740
  189.0 11.3 %copy-start.1 = (bf16[192,768]{1,0:T(8,128)(2,1)S(1)}, bf16[192,768]{1,0:T(8,128)(2,1)}, u32[]{:S(2)}) copy-start(bf16[192,768]{1,0:T(8,128)(2,1)} %param.15) | copy-start | bytes 884740

commit v3 on v2

--- a/solution.py
+++ b/solution.py
@@ -64,13 +64,19 @@
     )(part)
 
 
-def gather_slots(send_grads, send_rows):
+TRANSPOSED = (((1,), (1,)), ((), ()))
+STRIP = 256
+
+
+def gather_slots(send_grads, send_rows, down_matrix):
     experts, capacity, cols = send_rows.shape
     slots = experts * capacity
+    hidden = down_matrix.shape[0]
+    strips = hidden // STRIP
 
     def kernel(
-        grads_ref, rows_ref, out_grads, out_rows,
-        own_sem, z_send, z_recv, x_send, x_recv, m_send, m_recv, n_send, n_recv,
+        grads_ref, rows_ref, down_ref, out_grads, out_rows, out_act,
+        down_held, down_sem, own_sem, z_send, z_recv, x_send, x_recv, m_send, m_recv, n_send, n_recv,
     ):
         z = lax.axis_index("expert")
         t = lax.axis_index("tensor")
@@ -88,26 +94,20 @@
                 pl.ds(pl.multiple_of(quarter * cols, 128), cols),
             ]
 
-        z_copies = {}
-        for a in range(2):
-            for k in (2, 3, 1)[: experts - 1]:
-                copy = remote(
-                    ins[a].at[zs[k]], block(a, z, t), z_send.at[a, k], z_recv.at[a, k],
-                    {"expert": zs[k]},
-                )
-                copy.start()
-                z_copies[a, k] = copy
-        x_copies, m_copies, n_copies = {}, {}, {}
+        load_down = pltpu.make_async_copy(down_ref, down_held, down_sem)
+        load_down.start()
+        z_copies, x_copies, m_copies, n_copies = {}, {}, {}, {}
         quarter_x = lax.rem(t + 2, 4)
-        order = [(a, k) for a in range(2) for k in (0, 1, 3, 2)]
-
-        def pass_on(a, k):
-            far = block(a, from_z[k], quarter_x)
-            x_copies[a, k].wait_recv()
-            n_copies[a, k] = remote(far, far, n_send.at[a, k], n_recv.at[a, k], mate)
-            n_copies[a, k].start()
-
-        for i, (a, k) in enumerate(order):
+        sequence = (0, 1, 3, 2)
+
+        def send_z(a, k):
+            z_copies[a, k] = remote(
+                ins[a].at[zs[k]], block(a, z, t), z_send.at[a, k], z_recv.at[a, k],
+                {"expert": zs[k]},
+            )
+            z_copies[a, k].start()
+
+        def forward(a, k):
             near = block(a, from_z[k], t)
             if k == 0:
                 own = pltpu.make_async_copy(ins[a].at[z], near, own_sem.at[a])
@@ -115,106 +115,173 @@
                 own.wait()
             else:
                 z_copies[a, k].wait_recv()
+                if a == 0:
+                    send_z(1, k)
             x_copies[a, k] = remote(near, near, x_send.at[a, k], x_recv.at[a, k], over_x)
             x_copies[a, k].start()
             m_copies[a, k] = remote(near, near, m_send.at[a, k], m_recv.at[a, k], mate)
             m_copies[a, k].start()
+
+        def pass_on(a, k):
+            far = block(a, from_z[k], quarter_x)
+            x_copies[a, k].wait_recv()
+            n_copies[a, k] = remote(far, far, n_send.at[a, k], n_recv.at[a, k], mate)
+            n_copies[a, k].start()
+
+        def multiply(first, last):
+            @pl.loop(first, last)
+            def _(strip):
+                span = pl.ds(pl.multiple_of(strip * STRIP, STRIP), STRIP)
+                out_act[:, span] = lax.dot_general(
+                    out_grads[...], down_held[span, :], TRANSPOSED,
+                    preferred_element_type=jnp.float32,
+                )
+
+        for k in sequence[1:]:
+            send_z(0, k)
+        for i, k in enumerate(sequence):
+            forward(0, k)
             if i:
-                pass_on(*order[i - 1])
-        pass_on(*order[-1])
-        for group in (m_copies, n_copies):
-            for copy in group.values():
-                copy.wait_recv()
+                pass_on(0, sequence[i - 1])
+        forward(1, 0)
+        pass_on(0, sequence[-1])
+        for k in range(experts):
+            m_copies[0, k].wait_recv()
+            n_copies[0, k].wait_recv()
+        load_down.wait()
+        for i, k in enumerate(sequence[1:]):
+            forward(1, k)
+            pass_on(1, sequence[i])
+            multiply(strips * i // 4, strips * (i + 1) // 4)
+        pass_on(1, sequence[-1])
+        multiply(strips * 3 // 4, strips)
+        for k in range(experts):
+            m_copies[1, k].wait_recv()
+            n_copies[1, k].wait_recv()
         for group in (z_copies, x_copies, m_copies, n_copies):
             for copy in group.values():
                 copy.wait_send()
 
     sems = [pltpu.SemaphoreType.DMA((2, experts)) for _ in range(8)]
     shape = jax.ShapeDtypeStruct((slots, 4 * cols), send_rows.dtype)
+    vmem = pl.BlockSpec(memory_space=pltpu.VMEM)
     return pl.pallas_call(
         kernel,
-        out_shape=(shape, shape),
-        in_specs=[pl.BlockSpec(memory_space=pltpu.VMEM)] * 2,
-        out_specs=[pl.BlockSpec(memory_space=pltpu.VMEM)] * 2,
-        scratch_shapes=[pltpu.SemaphoreType.DMA((2,))] + sems,
+        out_shape=(shape, shape, jax.ShapeDtypeStruct((slots, hidden), jnp.float32)),
+        in_specs=[vmem, vmem, pl.BlockSpec(memory_space=pl.ANY)],
+        out_specs=[vmem] * 3,
+        scratch_shapes=[
+            pltpu.VMEM(down_matrix.shape, down_matrix.dtype),
+            pltpu.SemaphoreType.DMA,
+            pltpu.SemaphoreType.DMA((2,)),
+        ]
+        + sems,
         compiler_params=pltpu.CompilerParams(
-            collective_id=2, has_side_effects=True, vmem_limit_bytes=24 * 1024 * 1024
+            collective_id=2, has_side_effects=True, vmem_limit_bytes=50 * 1024 * 1024
         ),
-    )(send_grads, send_rows)
-
-
-def return_slots(row_part, scalars, experts, capacity, cols):
+    )(send_grads, send_rows, down_matrix)
+
+
+def return_slots(gate_grad, up_grad, gate_matrix, up_matrix, scalars, experts, capacity, cols):
+    width = gate_grad.shape[1]
+    half = 2 * capacity
+
     def kernel(
-        part_ref, scal_ref, out_rows, out_scal,
-        m_land, x_out, kept, x_land, z_out, s_land, s_x, s_xland, s_z,
-        m_send, m_recv, x_send, x_recv, z_send, z_recv,
+        gg_ref, ug_ref, gate_ref, up_ref, scal_ref, out_rows, out_scal,
+        lhs, held, part, m_out, m_land, x_out, x_land, z_out, s_land, s_x, s_xland, s_z,
+        w_sem, m_send, m_recv, x_send, x_recv, z_send, z_recv,
         sm_send, sm_recv, sx_send, sx_recv, sz_send, sz_recv,
     ):
         z = lax.axis_index("expert")
         t = lax.axis_index("tensor")
-        x_mine = t // 2
         core = lax.rem(t, 2)
-        over_x = {"tensor": lax.rem(t + 2, 4)}
-        mate = {"tensor": t + 1 - 2 * core}
+        t_x = lax.rem(t + 2, 4)
+        t_mate = t + 1 - 2 * core
+        over_x, mate = {"tensor": t_x}, {"tensor": t_mate}
         zs = [lax.rem(z + k, experts) for k in range(experts)]
         order = (2, 3, 1, 0)
+        quarters = (lax.rem(t_mate + 2, 4), t_x, t_mate, t)
+        loads = []
+        for n, quarter in enumerate(quarters):
+            span = pl.ds(pl.multiple_of(quarter * cols, cols), cols)
+            pair = [
+                pltpu.make_async_copy(ref.at[span, :], held.at[i, n], w_sem.at[i, n])
+                for i, ref in enumerate((gate_ref, up_ref))
+            ]
+            for load in pair:
+                load.start()
+            loads.append(pair)
         meet([over_x, mate] + [{"expert": zd} for zd in zs[1:]])
-
-        def rows(k):
-            return pl.ds(pl.multiple_of(zs[k] * capacity, capacity), capacity)
-
-        def lanes(quarter):
-            return pl.ds(pl.multiple_of(quarter * cols, 128), cols)
-
-        pending = []
         s_m = remote(scal_ref, s_land, sm_send, sm_recv, mate)
-        m_copies = {}
+        s_m.start()
         for n, k in enumerate(order):
-            for j in range(2):
-                xq = lax.rem(x_mine + 1 + j, 2)
-                m_copies[k, j] = remote(
-                    part_ref.at[rows(k), lanes(2 * xq + 1 - core)],
-                    m_land.at[k, j], m_send.at[k, j], m_recv.at[k, j], mate,
-                )
-                m_copies[k, j].start()
-            if n == 0:
-                s_m.start()
-        pending += list(m_copies.values()) + [s_m]
-        x_copies, z_copies = {}, {}
-        quarter_x = lax.rem(t + 2, 4)
-
-        def finish(k):
-            x_copies[k].wait_recv()
-            z_out[k] = (kept[k] + x_land[k].astype(jnp.float32)).astype(jnp.bfloat16)
-            if k:
-                z_copies[k] = remote(
-                    z_out.at[k], out_rows.at[z], z_send.at[k], z_recv.at[k], {"expert": zs[k]}
-                )
-                z_copies[k].start()
-            else:
-                out_rows[z] = z_out[0]
-
-        for n, k in enumerate(order):
-            m_copies[k, 0].wait_recv()
-            x_out[k] = (
-                part_ref[rows(k), lanes(quarter_x)].astype(jnp.float32)
-                + m_land[k, 0].astype(jnp.float32)
-            ).astype(jnp.bfloat16)
-            x_copies[k] = remote(x_out.at[k], x_land.at[k], x_send.at[k], x_recv.at[k], over_x)
-            x_copies[k].start()
-            if n == 0:
+            rows = pl.ds(pl.multiple_of(zs[k] * capacity, capacity), capacity)
+            lhs[0, n * capacity : (n + 1) * capacity, :] = gg_ref[rows, :]
+            lhs[1, n * capacity : (n + 1) * capacity, :] = ug_ref[rows, :]
+
+        def multiply(h, n):
+            if h == 0:
+                for load in loads[n]:
+                    load.wait()
+
+            @pl.loop(0, cols // STRIP)
+            def _(strip):
+                span = pl.ds(pl.multiple_of(strip * STRIP, STRIP), STRIP)
+                total = 0.0
+                for i in range(2):
+                    total = total + lax.dot_general(
+                        lhs[i, h * half : (h + 1) * half, :], held[i, n, span, :], TRANSPOSED,
+                        preferred_element_type=jnp.float32,
+                    )
+                if n in (0, 2):
+                    m_out[h, n // 2, :, span] = total.astype(jnp.bfloat16)
+                else:
+                    part[h, n // 2, :, span] = total
+
+        m_copies, x_copies, z_copies, s_copies = {}, {}, {}, []
+
+        def send_mate(h, j):
+            m_copies[h, j] = remote(
+                m_out.at[h, j], m_land.at[h, j], m_send.at[h, j], m_recv.at[h, j], mate
+            )
+            m_copies[h, j].start()
+
+        def finish(h):
+            m_copies[h, 1].wait_recv()
+            x_copies[h].wait_recv()
+            total = part[h, 1] + m_land[h, 1].astype(jnp.float32) + x_land[h].astype(jnp.float32)
+            z_out[h] = total.astype(jnp.bfloat16)
+            for i in range(2):
+                k = order[2 * h + i]
+                block = z_out.at[h, i * capacity : (i + 1) * capacity, :]
+                if k:
+                    z_copies[k] = remote(
+                        block, out_rows.at[z], z_send.at[k], z_recv.at[k], {"expert": zs[k]}
+                    )
+                    z_copies[k].start()
+                else:
+                    out_rows[z] = z_out[h, i * capacity : (i + 1) * capacity, :]
+
+        for h in range(2):
+            multiply(h, 0)
+            send_mate(h, 0)
+            if h == 1:
+                finish(0)
+            multiply(h, 1)
+            m_copies[h, 0].wait_recv()
+            x_out[h] = (part[h, 0] + m_land[h, 0].astype(jnp.float32)).astype(jnp.bfloat16)
+            x_copies[h] = remote(
+                x_out.at[h], x_land.at[h], x_send.at[h], x_recv.at[h], over_x
+            )
+            x_copies[h].start()
+            if h == 0:
                 s_m.wait_recv()
                 s_x[...] = scal_ref[...] + s_land[...]
                 s_xc = remote(s_x, s_xland, sx_send, sx_recv, over_x)
                 s_xc.start()
-                pending.append(s_xc)
-            m_copies[k, 1].wait_recv()
-            kept[k] = part_ref[rows(k), lanes(t)].astype(jnp.float32) + m_land[k, 1].astype(
-                jnp.float32
-            )
-            if n:
-                finish(order[n - 1])
-            if n == 1:
+            multiply(h, 2)
+            send_mate(h, 1)
+            if h == 0:
                 s_xc.wait_recv()
                 s_z[...] = s_x[...] + s_xland[...]
                 for j in range(1, experts):
@@ -223,44 +290,52 @@
                         {"expert": zs[j]},
                     )
                     copy.start()
-                    z_copies["s", j] = copy
+                    s_copies.append(copy)
                 out_scal[z] = s_z[z]
-        finish(order[-1])
-        for copy in z_copies.values():
+            multiply(h, 3)
+        finish(1)
+        for copy in list(z_copies.values()) + s_copies:
             copy.wait_recv()
-        for copy in pending + list(x_copies.values()) + list(z_copies.values()):
+        for copy in list(m_copies.values()) + list(x_copies.values()) + [s_m, s_xc]:
             copy.wait_send()
+        for copy in list(z_copies.values()) + s_copies:
+            copy.wait_send()
 
     f32, bf16, dma = jnp.float32, jnp.bfloat16, pltpu.SemaphoreType.DMA
-    chunk = (experts, capacity, cols)
+    vmem = pl.BlockSpec(memory_space=pltpu.VMEM)
+    anywhere = pl.BlockSpec(memory_space=pl.ANY)
     return pl.pallas_call(
         kernel,
         out_shape=(
-            jax.ShapeDtypeStruct(chunk, bf16),
+            jax.ShapeDtypeStruct((experts, capacity, cols), bf16),
             jax.ShapeDtypeStruct(scalars.shape, f32),
         ),
-        in_specs=[pl.BlockSpec(memory_space=pltpu.VMEM)] * 2,
-        out_specs=[pl.BlockSpec(memory_space=pltpu.VMEM)] * 2,
+        in_specs=[vmem, vmem, anywhere, anywhere, vmem],
+        out_specs=[vmem] * 2,
         scratch_shapes=[
-            pltpu.VMEM((experts, 2, capacity, cols), bf16),
-            pltpu.VMEM(chunk, bf16),
-            pltpu.VMEM(chunk, f32),
-            pltpu.VMEM(chunk, bf16),
-            pltpu.VMEM(chunk, bf16),
+            pltpu.VMEM((2, 2 * half, width), bf16),
+            pltpu.VMEM((2, 4, cols, width), bf16),
+            pltpu.VMEM((2, 2, half, cols), f32),
+            pltpu.VMEM((2, 2, half, cols), bf16),
+            pltpu.VMEM((2, 2, half, cols), bf16),
+            pltpu.VMEM((2, half, cols), bf16),
+            pltpu.VMEM((2, half, cols), bf16),
+            pltpu.VMEM((2, half, cols), bf16),
             pltpu.VMEM(scalars.shape, f32),
             pltpu.VMEM(scalars.shape, f32),
             pltpu.VMEM(scalars.shape, f32),
             pltpu.VMEM(scalars.shape, f32),
-            dma((experts, 2)), dma((experts, 2)),
-            dma((experts,)), dma((experts,)),
+            dma((2, 4)),
+            dma((2, 2)), dma((2, 2)),
+            dma((2,)), dma((2,)),
             dma((experts,)), dma((experts,)),
             dma, dma, dma, dma,
             dma((experts,)), dma((experts,)),
         ],
         compiler_params=pltpu.CompilerParams(
-            collective_id=3, has_side_effects=True, vmem_limit_bytes=32 * 1024 * 1024
+            collective_id=3, has_side_effects=True, vmem_limit_bytes=58 * 1024 * 1024
         ),
-    )(row_part, scalars)
+    )(gate_grad, up_grad, gate_matrix, up_matrix, scalars)
 
 
 def body(
@@ -270,7 +345,7 @@
     expert_count = router_weight.shape[1]
     feat_width = part_cols * lax.axis_size("tensor")
     capacity = 8 * tok_rows // (3 * expert_count)
-    direct = lax.axis_size("tensor") == 4 and expert_count == 4 and part_cols % 128 == 0
+    direct = lax.axis_size("tensor") == 4 and expert_count == 4 and part_cols % STRIP == 0 and down_weight.shape[1] % STRIP == 0
     inputs_f = hidden_in.astype(jnp.float32)
     scaled_in = inputs_f * norm_gain[None, :]
     square_part = jnp.sum(inputs_f * inputs_f, axis=1)
@@ -320,7 +395,7 @@
     send_rows = dispatch(pick_bf, normed_b)
     slot_total = expert_count * capacity
     if direct:
-        out_grad, slot_rows = gather_slots(send_grads, send_rows)
+        out_grad, slot_rows, act_grad = gather_slots(send_grads, send_rows, down_weight[0])
     else:
         got_rows = lax.all_to_all(send_rows, "expert", split_axis=0, concat_axis=0, tiled=True)
         got_grads = lax.all_to_all(send_grads, "expert", split_axis=0, concat_axis=0, tiled=True)
@@ -338,27 +413,30 @@
     grad_down = jnp.einsum(
         "sf,sd->fd", hidden_act, out_grad, preferred_element_type=jnp.float32
     ).astype(jnp.bfloat16)[None]
-    act_grad = jnp.einsum("sd,fd->sf", out_grad, down_matrix, preferred_element_type=jnp.float32)
+    if not direct:
+        act_grad = jnp.einsum("sd,fd->sf", out_grad, down_matrix, preferred_element_type=jnp.float32)
     gate_grad = (act_grad * up_pre * gate_sig * (1.0 + gate_pre * (1.0 - gate_sig))).astype(
         jnp.bfloat16
     )
     up_grad = (act_grad * gate_pre * gate_sig).astype(jnp.bfloat16)
-    row_part = jnp.einsum("sf,df->sd", gate_grad, gate_matrix, preferred_element_type=jnp.float32)
-    row_part = row_part + jnp.einsum(
-        "sf,df->sd", up_grad, up_matrix, preferred_element_type=jnp.float32
-    )
     prob_part = jnp.sum(hidden_act.astype(jnp.float32) * act_grad, axis=1)
     inner_part = jnp.sum(
         gate_grad.astype(jnp.float32) * gate_pre + up_grad.astype(jnp.float32) * up_pre, axis=1
     )
-    row_part = row_part.astype(jnp.bfloat16)
     if direct:
         scalars = jnp.stack([inner_part, prob_part], axis=0).reshape(2, expert_count, capacity)
         scalars = jnp.pad(scalars.transpose(1, 0, 2), ((0, 0), (0, 6), (0, 0)))
-        back_rows, scalars = return_slots(row_part, scalars, expert_count, capacity, part_cols)
+        back_rows, scalars = return_slots(
+            gate_grad, up_grad, gate_matrix, up_matrix, scalars, expert_count, capacity, part_cols
+        )
         back_rows = back_rows.reshape(slot_total, part_cols)
         scalars = scalars[:, :2].transpose(1, 0, 2).reshape(2, slot_total)
     else:
+        row_part = jnp.einsum("sf,df->sd", gate_grad, gate_matrix, preferred_element_type=jnp.float32)
+        row_part = row_part + jnp.einsum(
+            "sf,df->sd", up_grad, up_matrix, preferred_element_type=jnp.float32
+        )
+        row_part = row_part.astype(jnp.bfloat16)
         row_own = lax.psum_scatter(
             row_part, "tensor", scatter_dimension=1, tiled=True
         )

time: 201 us -> 171 us (0.85)
  matrix products: 84 us -> 43.9 us
  Pallas kernels: 104 us -> 113 us
    dot_general x3 -> x0, matrix products: 39.2 us -> none  [the longest x1 17.5 us: body(): jnp.einsum('sf,df->sd', gate_grad, gate_matrix, preferred_element_type=jn...]
    pallas_call x2, Pallas kernels: 91.1 us -> 99.9 us  [the longest x1 56.8 us: gather_slots(): pl.pallas_call(kernel, out_shape=(shape, shape, jax.ShapeDtypeStruct((slo...]
where the time goes in v3:
time: 171 us; the launch traced here: 170 us
  Pallas kernels  113 us (66%)
  matrix products  43.9 us (26%)
  other arithmetic  7.14 us (4%)
  local copies, waits for them, and re-layouts  5.63 us (3%)
    pallas_call x1, Pallas kernels, gather_slots(): pl.pallas_call(kernel, out_shape=(shape, shape, jax.ShapeDtypeStruct((slo...  56.8 us
    pallas_call x1, Pallas kernels, return_slots(): pl.pallas_call(kernel, out_shape=(jax.ShapeDtypeStruct((experts, capacity...  43.2 us
    dot_general x1, matrix products, body(): up_pre = jnp.dot(slot_rows, up_matrix, preferred_element_type=jnp.float32)  15 us
    pallas_call x2, Pallas kernels, small_psum(): pl.pallas_call(kernel, out_shape=jax.ShapeDtypeStruct(part.shape, part.dt...  12.9 us
    dot_general x1, matrix products, body(): jnp.einsum('sf,sd->fd', hidden_act, out_grad, preferred_element_type=jnp....  11.6 us
    dot_general x1, matrix products, body(): jnp.dot(slot_rows, gate_matrix, preferred_element_type=jnp.float32)  9.71 us

profile of v3, /device:TPU:0, one launch (start us, length us, event | category | flops | bytes accessed | tf_op | source)
XLA Modules:
  0.0 170.4 jit_solution(11497440703223646997)
XLA Ops:
  0.6 0.0 copy-start
  0.6 0.0 copy-start.4
  0.7 0.0 copy-start.8
  0.7 1.6 convolution_bitcast_fusion
  2.3 1.1 fusion.4
  3.4 0.6 select_maximum_fusion.1.part_ref
  4.0 5.9 %shard_map.111 = f32[8,256]{1,0:T(8,128)} custom-call(f32[8,256]{1,0:T(8,128)} %select_maximum_fusion.1.part_ref), custom_call_target="tpu_custom_call" | custom-call | tf_op jit(solution)/shard_map/pallas_call | solution.py:53
  9.9 0.7 fusion.49
  10.6 0.8 copy.20
  11.4 0.1 eq.103
  11.6 1.2 reduce-window.6
  12.8 0.2 slice_reduce_fusion
  13.0 0.2 reduce-window.9
  13.2 0.1 add_bitcast_fusion
  13.3 0.1 eq.99
  13.5 0.1 reduce_sum.67
  13.6 0.1 copy.22
  13.7 0.7 multiply_add_fusion
  14.4 0.1 fusion.10
  14.5 0.9 pad_maximum_fusion
  15.5 0.8 fusion.52
  16.2 0.7 fusion.29
  17.0 0.0 copy-done
  17.0 0.5 convolution_convert_fusion.1
  17.5 0.0 copy-done.4
  17.5 0.0 copy-done.8
  17.5 0.5 convolution_convert_fusion
  18.1 0.0 copy-start.2
  18.1 56.8 %shard_map.112 = (bf16[512,3072]{1,0:T(8,128)(2,1)}, bf16[512,3072]{1,0:T(8,128)(2,1)}, f32[512,2048]{1,0:T(8,128)}) custom-call(bf16[4,128,768]{2,1,0:T(8,128)(2,1)S(1)} %bitcast.75, bf16[4,128,768]{2,1,0:T(8,128)(2,1)S(1)} %bitcast.76, bf16[2048,3072]{1,0:T(8,128)(2,1)} %bitcast.77), custom_call_target="tpu_custom_call" | custom-call | tf_op jit(solution)/shard_map/pallas_call | solution.py:168
  74.9 0.0 copy-done.2
  74.9 0.0 copy-start.9
  74.9 9.7 %fusion.44 = f32[512,2048]{1,0:T(8,128)} fusion(bf16[512,3072]{1,0:T(8,128)(2,1)} %get-tuple-element.10, bf16[1,3072,2048]{2,1,0:T(8,128)(2,1)S(1)} %copy-done.2), kind=kOutput, calls=%fused_computation.92 | convolution fusion | flops 6442450944 | bytes 19922944 | tf_op jit(solution)/shard_map/dot_general | solution.py:409
  84.6 0.0 copy-done.9
  84.6 15.0 %multiply_reduce_fusion = (f32[512]{0:T(512)S(1)}, bf16[512,2048]{1,0:T(8,128)(2,1)S(1)}, f32[512]{0:T(512)S(1)}, bf16[512,2048]{1,0:T(8,128)(2,1)}, bf16[512,2048]{1,0:T(8,128)(2,1)}) fusion(f32[512,2048]{1,0:T(8,128)S(1)} %copy-done.9, f32[512,2048]{1,0:T(8,128)} %fusion.44, bf16[512,3072]{1,0:T(8,128)(2,1)} %get-tuple-element.10, ...), kind=kOutput, calls=%fused_computation.1 | convolution fusion | flops 6468664320 | bytes 30412800 | tf_op jit(solution)/shard_map/dot_general | solution.py:410
  99.6 0.6 pad.13.scal_ref
  100.2 0.0 copy-start.3
  100.2 0.0 copy-start.7
  100.2 0.0 copy-start.6
  100.2 0.0 copy-start.5
  100.2 43.2 %shard_map.113 = (bf16[4,128,768]{2,1,0:T(8,128)(2,1)}, f32[4,8,128]{2,1,0:T(8,128)}) custom-call(bf16[512,2048]{1,0:T(8,128)(2,1)} %get-tuple-element.23.gg_ref, bf16[512,2048]{1,0:T(8,128)(2,1)} %get-tuple-element.22.ug_ref, bf16[3072,2048]{1,0:T(8,128)(2,1)} %bitcast.78, bf16[3072,2048]{1,0:T(8,128)(2,1)} %bitcast.79, f32[4,8,128]{2,1,0:T(8,128)} %pad.13.scal_ref), custom_call_target="tpu_custom_call" | custom-call | tf_op jit(solution)/shard_map/pallas_call | solution.py:307
  143.4 0.0 copy-done.3
  143.4 1.5 fusion.27
  144.9 0.0 copy-done.7
  145.0 0.0 copy-done.6
  145.0 0.7 fusion.34
  145.7 0.0 copy-done.5
  145.7 2.3 %fusion.9 = (f32[768]{0:T(1024)S(1)}, bf16[192,768]{1,0:T(8,128)(2,1)}) fusion(bf16[192,768]{1,0:T(8,128)(2,1)S(1)} %copy-done.5, f32[192]{0:T(256)S(1)} %bitcast.93, f32[192]{0:T(256)S(1)} %multiply_multiply_fusion.1, f32[192]{0:T(256)S(1)} %multiply_multiply_fusion, f32[768]{0:T(1024)S(1)} %copy-done.8, f32[192,768]{1,0:T(8,128)S(1)} %fusion.34, ...), kind=kOutput, calls=%fused_computation.24 | convolution fusion | flops 153206016 | bytes 1976064 | tf_op jit(solution)/shard_map/dot_general | solution.py:454
  148.0 0.5 fusion.1
  148.5 0.6 select_maximum_fusion.part_ref
  149.1 7.0 %shard_map.114 = f32[8,768]{1,0:T(8,128)} custom-call(f32[8,768]{1,0:T(8,128)} %select_maximum_fusion.part_ref), custom_call_target="tpu_custom_call" | custom-call | tf_op jit(solution)/shard_map/pallas_call | solution.py:53
  156.1 1.3 slice_reduce_fusion.1
  157.5 1.3 slice_bitcast_fusion
  158.8 0.0 copy-start.1
  158.8 11.6 %convert_bitcast_fusion = bf16[1,2048,3072]{2,1,0:T(8,128)(2,1)} fusion(bf16[512,2048]{1,0:T(8,128)(2,1)S(1)} %get-tuple-element.18, bf16[512,3072]{1,0:T(8,128)(2,1)} %get-tuple-element.13), kind=kOutput, calls=%fused_computation | convolution fusion | flops 6448742400 | bytes 17825792 | tf_op jit(solution)/shard_map/sf,sd->fd/dot_general | solution.py:413
  170.4 0.0 copy-done.1
  (12 shorter events, 0.1 us)
Async XLA Ops:
  0.6 16.3 %copy-start = (bf16[192,768]{1,0:T(8,128)(2,1)S(1)}, bf16[192,768]{1,0:T(8,128)(2,1)}, u32[]{:S(2)}) copy-start(bf16[192,768]{1,0:T(8,128)(2,1)} %param.15) | copy-start | bytes 884740
  0.6 16.9 %copy-start.4 = (bf16[192,768]{1,0:T(8,128)(2,1)S(1)}, bf16[192,768]{1,0:T(8,128)(2,1)}, u32[]{:S(2)}) copy-start(bf16[192,768]{1,0:T(8,128)(2,1)} %param.8) | copy-start | bytes 884740
  0.7 16.9 %copy-start.8 = (f32[768]{0:T(1024)S(1)}, f32[768]{0:T(1024)}, u32[]{:S(2)}) copy-start(f32[768]{0:T(1024)} %param.9) | copy-start | bytes 9220
  18.1 56.8 %copy-start.2 = (bf16[1,3072,2048]{2,1,0:T(8,128)(2,1)S(1)}, bf16[1,3072,2048]{2,1,0:T(8,128)(2,1)}, u32[]{:S(2)}) copy-start(bf16[1,3072,2048]{2,1,0:T(8,128)(2,1)} %param.12) | copy-start | bytes 37748740
  74.9 9.7 %copy-start.9 = (f32[512,2048]{1,0:T(8,128)S(1)}, f32[512,2048]{1,0:T(8,128)}, u32[]{:S(2)}) copy-start(f32[512,2048]{1,0:T(8,128)} %get-tuple-element.9) | copy-start | bytes 12582916
  100.2 43.2 %copy-start.3 = (f32[384,512]{1,0:T(8,128)S(1)}, f32[384,512]{1,0:T(8,128)}, u32[]{:S(2)}) copy-start(f32[384,512]{1,0:T(8,128)} %pad_maximum_fusion) | copy-start | bytes 2359300
  100.2 44.7 %copy-start.7 = (f32[8,256]{1,0:T(8,128)S(1)}, f32[8,256]{1,0:T(8,128)}, u32[]{:S(2)}) copy-start(f32[8,256]{1,0:T(8,128)} %shard_map.111) | copy-start | bytes 24580
  100.2 44.8 %copy-start.6 = (f32[768,4]{0,1:T(4,128)S(1)}, f32[768,4]{0,1:T(4,128)}, u32[]{:S(2)}) copy-start(f32[768,4]{0,1:T(4,128)} %param.10) | copy-start | bytes 36868
  100.2 45.5 %copy-start.5 = (bf16[192,768]{1,0:T(8,128)(2,1)S(1)}, bf16[192,768]{1,0:T(8,128)(2,1)}, u32[]{:S(2)}) copy-start(bf16[192,768]{1,0:T(8,128)(2,1)} %param.8) | copy-start | bytes 884740
  158.8 11.6 %copy-start.1 = (bf16[192,768]{1,0:T(8,128)(2,1)S(1)}, bf16[192,768]{1,0:T(8,128)(2,1)}, u32[]{:S(2)}) copy-start(bf16[192,768]{1,0:T(8,128)(2,1)} %param.15) | copy-start | bytes 884740

commit v4 on v3

--- a/solution.py
+++ b/solution.py
@@ -68,15 +68,15 @@
 STRIP = 256
 
 
-def gather_slots(send_grads, send_rows, down_matrix):
+def gather_slots(send_grads, send_rows, down_matrix, gate_matrix):
     experts, capacity, cols = send_rows.shape
     slots = experts * capacity
     hidden = down_matrix.shape[0]
     strips = hidden // STRIP
 
     def kernel(
-        grads_ref, rows_ref, down_ref, out_grads, out_rows, out_act,
-        down_held, down_sem, own_sem, z_send, z_recv, x_send, x_recv, m_send, m_recv, n_send, n_recv,
+        grads_ref, rows_ref, down_ref, gate_ref, out_grads, out_rows, out_act, out_gate,
+        down_held, gate_held, lhs, down_sem, gate_sem, own_sem, z_send, z_recv, x_send, x_recv, m_send, m_recv, n_send, n_recv,
     ):
         z = lax.axis_index("expert")
         t = lax.axis_index("tensor")
@@ -96,6 +96,8 @@
 
         load_down = pltpu.make_async_copy(down_ref, down_held, down_sem)
         load_down.start()
+        load_gate = pltpu.make_async_copy(gate_ref, gate_held, gate_sem)
+        load_gate.start()
         z_copies, x_copies, m_copies, n_copies = {}, {}, {}, {}
         quarter_x = lax.rem(t + 2, 4)
         sequence = (0, 1, 3, 2)
@@ -136,6 +138,22 @@
                     out_grads[...], down_held[span, :], TRANSPOSED,
                     preferred_element_type=jnp.float32,
                 )
+
+        def project(pair):
+            for i, k in enumerate(pair):
+                m_copies[1, k].wait_recv()
+                n_copies[1, k].wait_recv()
+                lhs[i * capacity : (i + 1) * capacity, :] = out_rows[source_rows(k), :]
+
+            @pl.loop(0, strips)
+            def _(strip):
+                span = pl.ds(pl.multiple_of(strip * STRIP, STRIP), STRIP)
+                total = jnp.dot(lhs[...], gate_held[:, span], preferred_element_type=jnp.float32)
+                for i, k in enumerate(pair):
+                    out_gate[source_rows(k), span] = total[i * capacity : (i + 1) * capacity]
+
+        def source_rows(k):
+            return pl.ds(pl.multiple_of(from_z[k] * capacity, capacity), capacity)
 
         for k in sequence[1:]:
             send_z(0, k)
@@ -152,12 +170,12 @@
         for i, k in enumerate(sequence[1:]):
             forward(1, k)
             pass_on(1, sequence[i])
-            multiply(strips * i // 4, strips * (i + 1) // 4)
+            if i < 2:
+                multiply(strips * i // 2, strips * (i + 1) // 2)
+        load_gate.wait()
+        project(sequence[:2])
         pass_on(1, sequence[-1])
-        multiply(strips * 3 // 4, strips)
-        for k in range(experts):
-            m_copies[1, k].wait_recv()
-            n_copies[1, k].wait_recv()
+        project(sequence[2:])
         for group in (z_copies, x_copies, m_copies, n_copies):
             for copy in group.values():
                 copy.wait_send()
@@ -167,19 +185,22 @@
     vmem = pl.BlockSpec(memory_space=pltpu.VMEM)
     return pl.pallas_call(
         kernel,
-        out_shape=(shape, shape, jax.ShapeDtypeStruct((slots, hidden), jnp.float32)),
-        in_specs=[vmem, vmem, pl.BlockSpec(memory_space=pl.ANY)],
-        out_specs=[vmem] * 3,
+        out_shape=(shape, shape) + (jax.ShapeDtypeStruct((slots, hidden), jnp.float32),) * 2,
+        in_specs=[vmem, vmem] + [pl.BlockSpec(memory_space=pl.ANY)] * 2,
+        out_specs=[vmem] * 4,
         scratch_shapes=[
             pltpu.VMEM(down_matrix.shape, down_matrix.dtype),
+            pltpu.VMEM(gate_matrix.shape, gate_matrix.dtype),
+            pltpu.VMEM((2 * capacity, 4 * cols), send_rows.dtype),
+            pltpu.SemaphoreType.DMA,
             pltpu.SemaphoreType.DMA,
             pltpu.SemaphoreType.DMA((2,)),
         ]
         + sems,
         compiler_params=pltpu.CompilerParams(
-            collective_id=2, has_side_effects=True, vmem_limit_bytes=50 * 1024 * 1024
+            collective_id=2, has_side_effects=True, vmem_limit_bytes=58 * 1024 * 1024
         ),
-    )(send_grads, send_rows, down_matrix)
+    )(send_grads, send_rows, down_matrix, gate_matrix)
 
 
 def return_slots(gate_grad, up_grad, gate_matrix, up_matrix, scalars, experts, capacity, cols):
@@ -395,7 +416,9 @@
     send_rows = dispatch(pick_bf, normed_b)
     slot_total = expert_count * capacity
     if direct:
-        out_grad, slot_rows, act_grad = gather_slots(send_grads, send_rows, down_weight[0])
+        out_grad, slot_rows, act_grad, gate_pre = gather_slots(
+            send_grads, send_rows, down_weight[0], gate_weight[0]
+        )
     else:
         got_rows = lax.all_to_all(send_rows, "expert", split_axis=0, concat_axis=0, tiled=True)
         got_grads = lax.all_to_all(send_grads, "expert", split_axis=0, concat_axis=0, tiled=True)
@@ -406,7 +429,8 @@
     gate_matrix = gate_weight[0]
     up_matrix = up_weight[0]
     down_matrix = down_weight[0]
-    gate_pre = jnp.dot(slot_rows, gate_matrix, preferred_element_type=jnp.float32)
+    if not direct:
+        gate_pre = jnp.dot(slot_rows, gate_matrix, preferred_element_type=jnp.float32)
     up_pre = jnp.dot(slot_rows, up_matrix, preferred_element_type=jnp.float32)
     gate_sig = jax.nn.sigmoid(gate_pre)
     hidden_act = (gate_pre * gate_sig * up_pre).astype(jnp.bfloat16)

time: 171 us -> 173 us (1.012)
  Pallas kernels: 113 us -> 122 us
  matrix products: 43.9 us -> 37 us
    dot_general x1 -> x0, matrix products: 9.71 us -> none  [body(): jnp.dot(slot_rows, gate_matrix, preferred_element_type=jnp.float32)]
    pallas_call x1, Pallas kernels: 56.8 us -> 64.3 us  [gather_slots(): pl.pallas_call(kernel, out_shape=(shape, shape) + (jax.ShapeDtypeStruct((...]
    dot_general x2, matrix products: 1.06 us -> 2.84 us  [dispatch(): jnp.einsum('ts,td->sd', pick, row_block, preferred_element_type=jnp.float32)]
    pallas_call x1, Pallas kernels: 43.2 us -> 44.9 us  [return_slots(): pl.pallas_call(kernel, out_shape=(jax.ShapeDtypeStruct((experts, capacity...]
where the time goes in v4:
time: 173 us; the launch traced here: 172 us
  Pallas kernels  122 us (71%)
  matrix products  37 us (21%)
  other arithmetic  6.26 us (4%)
  local copies, waits for them, and re-layouts  5.62 us (3%)
    pallas_call x1, Pallas kernels, gather_slots(): pl.pallas_call(kernel, out_shape=(shape, shape) + (jax.ShapeDtypeStruct((...  64.3 us
    pallas_call x1, Pallas kernels, return_slots(): pl.pallas_call(kernel, out_shape=(jax.ShapeDtypeStruct((experts, capacity...  44.9 us
    dot_general x1, matrix products, body(): up_pre = jnp.dot(slot_rows, up_matrix, preferred_element_type=jnp.float32)  16 us
    pallas_call x2, Pallas kernels, small_psum(): pl.pallas_call(kernel, out_shape=jax.ShapeDtypeStruct(part.shape, part.dt...  12.9 us
    dot_general x1, matrix products, body(): jnp.einsum('sf,sd->fd', hidden_act, out_grad, preferred_element_type=jnp....  11.6 us

profile of v4, /device:TPU:0, one launch (start us, length us, event | category | flops | bytes accessed | tf_op | source)
XLA Modules:
  0.0 171.9 jit_solution(8252008649587112375)
XLA Ops:
  0.6 0.0 copy-start
  0.6 0.0 copy-start.2
  0.7 0.0 copy-start.5
  0.7 1.6 convolution_bitcast_fusion
  2.3 1.1 fusion.4
  3.4 0.6 select_maximum_fusion.1.part_ref
  4.0 5.9 %shard_map.111 = f32[8,256]{1,0:T(8,128)} custom-call(f32[8,256]{1,0:T(8,128)} %select_maximum_fusion.1.part_ref), custom_call_target="tpu_custom_call" | custom-call | tf_op jit(solution)/shard_map/pallas_call | solution.py:53
  9.9 0.7 fusion.47
  10.6 0.8 copy.20
  11.4 0.1 eq.103
  11.6 1.2 reduce-window.6
  12.8 0.2 slice_reduce_fusion
  13.0 0.2 reduce-window.9
  13.2 0.1 add_bitcast_fusion
  13.3 0.1 eq.99
  13.5 0.1 reduce_sum.67
  13.6 0.1 copy.22
  13.7 0.7 multiply_add_fusion
  14.4 0.1 fusion.10
  14.5 0.1 pad_maximum_fusion
  14.6 0.8 fusion.50
  15.3 0.7 fusion.29
  16.1 0.0 copy-done
  16.1 1.4 convolution_convert_fusion.1
  17.5 0.0 copy-done.2
  17.5 0.0 copy-done.5
  17.5 1.4 convolution_convert_fusion
  18.9 64.3 %shard_map.112 = (bf16[512,3072]{1,0:T(8,128)(2,1)}, bf16[512,3072]{1,0:T(8,128)(2,1)}, f32[512,2048]{1,0:T(8,128)}, f32[512,2048]{1,0:T(8,128)}) custom-call(bf16[4,128,768]{2,1,0:T(8,128)(2,1)} %bitcast.77, bf16[4,128,768]{2,1,0:T(8,128)(2,1)} %bitcast.78, bf16[2048,3072]{1,0:T(8,128)(2,1)} %bitcast.74, bf16[3072,2048]{1,0:T(8,128)(2,1)} %bitcast.72), custom_call_target="tpu_custom_call" | custom-call | tf_op jit(solution)/shard_map/pallas_call | solution.py:186
  83.2 16.0 %multiply_reduce_fusion = (f32[512]{0:T(512)S(1)}, bf16[512,2048]{1,0:T(8,128)(2,1)S(1)}, f32[512]{0:T(512)S(1)}, bf16[512,2048]{1,0:T(8,128)(2,1)}, bf16[512,2048]{1,0:T(8,128)(2,1)}) fusion(f32[512,2048]{1,0:T(8,128)} %get-tuple-element.10, f32[512,2048]{1,0:T(8,128)} %get-tuple-element.12, bf16[512,3072]{1,0:T(8,128)(2,1)} %get-tuple-element.11, ...), kind=kOutput, calls=%fused_computation.1 | convolution fusion | flops 6468664320 | bytes 30412800 | tf_op jit(solution)/shard_map/dot_general | solution.py:434
  99.2 0.6 pad.13.scal_ref
  99.9 0.0 copy-start.4
  99.9 0.0 copy-start.3
  99.9 44.9 %shard_map.113 = (bf16[4,128,768]{2,1,0:T(8,128)(2,1)}, f32[4,8,128]{2,1,0:T(8,128)}) custom-call(bf16[512,2048]{1,0:T(8,128)(2,1)} %get-tuple-element.25.gg_ref, bf16[512,2048]{1,0:T(8,128)(2,1)} %get-tuple-element.24.ug_ref, bf16[3072,2048]{1,0:T(8,128)(2,1)} %bitcast.73, bf16[3072,2048]{1,0:T(8,128)(2,1)} %bitcast.75, f32[4,8,128]{2,1,0:T(8,128)} %pad.13.scal_ref), custom_call_target="tpu_custom_call" | custom-call | tf_op jit(solution)/shard_map/pallas_call | solution.py:328
  144.8 1.5 fusion.27
  146.3 0.0 copy-done.4
  146.4 0.0 copy-done.3
  146.4 0.7 fusion.34
  147.1 2.3 %fusion.9 = (f32[768]{0:T(1024)S(1)}, bf16[192,768]{1,0:T(8,128)(2,1)}) fusion(bf16[192,768]{1,0:T(8,128)(2,1)S(1)} %copy-done.2, f32[192]{0:T(256)S(1)} %bitcast.91, f32[192]{0:T(256)S(1)} %multiply_multiply_fusion.1, f32[192]{0:T(256)S(1)} %multiply_multiply_fusion, f32[768]{0:T(1024)S(1)} %copy-done.5, f32[192,768]{1,0:T(8,128)S(1)} %fusion.34, ...), kind=kOutput, calls=%fused_computation.24 | convolution fusion | flops 153206016 | bytes 1976064 | tf_op jit(solution)/shard_map/dot_general | solution.py:478
  149.4 0.5 fusion.1
  149.9 0.6 select_maximum_fusion.part_ref
  150.5 7.0 %shard_map.114 = f32[8,768]{1,0:T(8,128)} custom-call(f32[8,768]{1,0:T(8,128)} %select_maximum_fusion.part_ref), custom_call_target="tpu_custom_call" | custom-call | tf_op jit(solution)/shard_map/pallas_call | solution.py:53
  157.5 1.3 slice_reduce_fusion.1
  158.9 1.3 slice_bitcast_fusion
  160.2 0.0 copy-start.1
  160.2 11.6 %convert_bitcast_fusion = bf16[1,2048,3072]{2,1,0:T(8,128)(2,1)} fusion(bf16[512,2048]{1,0:T(8,128)(2,1)S(1)} %get-tuple-element.20, bf16[512,3072]{1,0:T(8,128)(2,1)} %get-tuple-element.15), kind=kOutput, calls=%fused_computation | convolution fusion | flops 6448742400 | bytes 17825792 | tf_op jit(solution)/shard_map/sf,sd->fd/dot_general | solution.py:437
  171.9 0.0 copy-done.1
  (12 shorter events, 0.1 us)
Async XLA Ops:
  0.6 15.5 %copy-start = (bf16[192,768]{1,0:T(8,128)(2,1)S(1)}, bf16[192,768]{1,0:T(8,128)(2,1)}, u32[]{:S(2)}) copy-start(bf16[192,768]{1,0:T(8,128)(2,1)} %param.15) | copy-start | bytes 884740
  0.6 16.9 %copy-start.2 = (bf16[192,768]{1,0:T(8,128)(2,1)S(1)}, bf16[192,768]{1,0:T(8,128)(2,1)}, u32[]{:S(2)}) copy-start(bf16[192,768]{1,0:T(8,128)(2,1)} %param.8) | copy-start | bytes 884740
  0.7 16.9 %copy-start.5 = (f32[768]{0:T(1024)S(1)}, f32[768]{0:T(1024)}, u32[]{:S(2)}) copy-start(f32[768]{0:T(1024)} %param.9) | copy-start | bytes 9220
  99.9 46.4 %copy-start.4 = (f32[8,256]{1,0:T(8,128)S(1)}, f32[8,256]{1,0:T(8,128)}, u32[]{:S(2)}) copy-start(f32[8,256]{1,0:T(8,128)} %shard_map.111) | copy-start | bytes 24580
  99.9 46.5 %copy-start.3 = (f32[768,4]{0,1:T(4,128)S(1)}, f32[768,4]{0,1:T(4,128)}, u32[]{:S(2)}) copy-start(f32[768,4]{0,1:T(4,128)} %param.10) | copy-start | bytes 36868
  160.2 11.7 %copy-start.1 = (bf16[192,768]{1,0:T(8,128)(2,1)S(1)}, bf16[192,768]{1,0:T(8,128)(2,1)}, u32[]{:S(2)}) copy-start(bf16[192,768]{1,0:T(8,128)(2,1)} %param.15) | copy-start | bytes 884740
